TPU v7x, 512 devices: a whole 4x4x16 slice. The times are simulated.
512 devices in a mesh: grp: 16 (over y_hi, x, core), inner: 32 (over z, y_lo).
Axes of the slice: x: 4, y: 4 (y_hi: 2, y_lo: 2; y = y_hi * 2 + y_lo), z: 16, core: 2. Of those that a mesh axis runs over, the one named last changes fastest.
Arguments:
- tokens: bfloat16 [256, 128, 8, 512], P('grp', 'inner'), may hold values from -6 to 6
- conv_weight: bfloat16 [27, 512], replicated, may hold values from -0.59765625 to 0.59765625
- gain: float32 [512], replicated, may hold values from 0.1 to 1.9
- bands: int32 [4, 2], replicated, may hold values from 0 to 3, as said below
- w_query: bfloat16 [512, 512], replicated, may hold values from -1 to 1
- w_key: bfloat16 [512, 512], replicated, may hold values from -1 to 1
- w_value: bfloat16 [512, 512], replicated, may hold values from -0.25 to 0.25
- w_out: bfloat16 [512, 512], replicated, may hold values from -0.25 to 0.25
- grad_out: bfloat16 [256, 128, 8, 512], P('grp', 'inner'), may hold values from -6 to 6
Outputs:
- output: bfloat16 [256, 128, 8, 512], P('grp', 'inner')
- grad_tokens: bfloat16 [256, 128, 8, 512], P('grp', 'inner')
Inputs may be any that keep to these rules, and one draw needn't show every extreme that they name: bands[i, 0] and bands[i, 1] count key blocks of 64 tokens below and above query block i.
All inputs are finite; a program needn't handle non-finite values.
Results may differ from a plain program's by a relative error of at most 0.013.
Values may be sent and summed in bfloat16 or wider, within the bound.
A program may use at most 64 MiB of HBM per device.

v0:
```python
import math

import jax
import jax.numpy as jnp
from jax import lax
from jax.sharding import PartitionSpec as P

HEADS = 8
HEAD_DIM = 64


def padded_2(cells, sides, width):
    for axis, dim in sides:
        count = lax.axis_size(axis)
        ends = count - 1
        head = lax.slice_in_dim(cells, 0, width, axis=dim)
        tail = lax.slice_in_dim(cells, cells.shape[dim] - width, cells.shape[dim], axis=dim)
        cells = jnp.concatenate(
            [
                lax.ppermute(tail, axis, [(i, (i + 1) % count) for i in range(ends)]),
                cells,
                lax.ppermute(head, axis, [((i + 1) % count, i) for i in range(ends)]),
            ],
            axis=dim,
        )
    return cells


def conv_forward(padded, taps):
    dep = padded.shape[0] - 2
    hgt = padded.shape[1] - 2
    wid = padded.shape[2] - 2
    total = jnp.zeros((dep, hgt, wid, padded.shape[3]), jnp.float32)
    for first in range(3):
        for second in range(3):
            for third in range(3):
                tap = taps[first * 9 + second * 3 + third]
                total = total + tap * padded[
                    first : first + dep, second : second + hgt, third : third + wid
                ].astype(jnp.float32)
    return total


def conv_adjoint(padded, taps):
    dep = padded.shape[0] - 2
    hgt = padded.shape[1] - 2
    wid = padded.shape[2] - 2
    total = jnp.zeros((dep, hgt, wid, padded.shape[3]), jnp.float32)
    for first in range(3):
        for second in range(3):
            for third in range(3):
                tap = taps[first * 9 + second * 3 + third]
                total = total + tap * padded[
                    2 - first : 2 - first + dep,
                    2 - second : 2 - second + hgt,
                    2 - third : 2 - third + wid,
                ].astype(jnp.float32)
    return total


def layer_norm(filtered, gain):
    values = filtered.astype(jnp.float32)
    centred = values - jnp.mean(values, -1, keepdims=True)
    scale = lax.rsqrt(jnp.mean(centred * centred, -1, keepdims=True) + 1e-05)
    return centred * scale * gain


def layer_norm_back(filtered, gain, grad_normed):
    values = filtered.astype(jnp.float32)
    centred = values - jnp.mean(values, -1, keepdims=True)
    scale = lax.rsqrt(jnp.mean(centred * centred, -1, keepdims=True) + 1e-05)
    unit = centred * scale
    scaled = grad_normed.astype(jnp.float32) * gain
    return scale * (
        scaled
        - jnp.mean(scaled, -1, keepdims=True)
        - unit * jnp.mean(scaled * unit, -1, keepdims=True)
    )


def band_mask(bands, length):
    blocks = bands.shape[0]
    block_len = length // blocks
    query_block = jnp.arange(length, dtype=jnp.int32) // block_len
    onehot = (query_block[:, None] == jnp.arange(blocks, dtype=jnp.int32)[None, :]).astype(
        jnp.int32
    )
    lower = jnp.sum(onehot * bands[None, :, 0], 1)
    upper = jnp.sum(onehot * bands[None, :, 1], 1)
    low_edge = (query_block - lower)[:, None]
    high_edge = (query_block + upper)[:, None]
    return (query_block[None, :] >= low_edge) & (query_block[None, :] <= high_edge)


def softmax_probs(query_heads, key_heads, bands):
    length = query_heads.shape[0]
    scores = jnp.einsum(
        "qchd,kchd->chqk", query_heads, key_heads, preferred_element_type=jnp.float32
    ) * (1.0 / math.sqrt(HEAD_DIM))
    allowed = band_mask(bands, length)
    masked = jnp.where(allowed, scores, -1e30)
    top = jnp.max(masked, -1, keepdims=True)
    expo = jnp.where(allowed, jnp.exp(masked - top), 0.0)
    return expo / jnp.sum(expo, -1, keepdims=True)


def attend(query, keys, values, bands):
    length, cols = (query.shape[0], query.shape[1])
    shape = (length, cols, HEADS, HEAD_DIM)
    query_heads, key_heads, value_heads = (
        query.reshape(shape),
        keys.reshape(shape),
        values.reshape(shape),
    )
    weights = softmax_probs(query_heads, key_heads, bands).astype(jnp.bfloat16)
    result = jnp.einsum("chqk,kchd->qchd", weights, value_heads, preferred_element_type=jnp.float32)
    return result.astype(jnp.bfloat16).reshape(length, cols, HEADS * HEAD_DIM)


def attend_back(query, keys, values, grad_att, bands):
    length, cols = (query.shape[0], query.shape[1])
    shape = (length, cols, HEADS, HEAD_DIM)
    query_heads, key_heads, value_heads = (
        query.reshape(shape),
        keys.reshape(shape),
        values.reshape(shape),
    )
    grad_heads = grad_att.reshape(shape)
    probs = softmax_probs(query_heads, key_heads, bands)
    weights = probs.astype(jnp.bfloat16)
    grad_probs = jnp.einsum(
        "qchd,kchd->chqk", grad_heads, value_heads, preferred_element_type=jnp.float32
    )
    grad_value = jnp.einsum(
        "chqk,qchd->kchd", weights, grad_heads, preferred_element_type=jnp.float32
    ).astype(jnp.bfloat16)
    centre = jnp.sum(probs * grad_probs, -1, keepdims=True)
    grad_scores = (probs * (grad_probs - centre) * (1.0 / math.sqrt(HEAD_DIM))).astype(jnp.bfloat16)
    grad_query = jnp.einsum(
        "chqk,kchd->qchd", grad_scores, key_heads, preferred_element_type=jnp.float32
    ).astype(jnp.bfloat16)
    grad_key = jnp.einsum(
        "chqk,qchd->kchd", grad_scores, query_heads, preferred_element_type=jnp.float32
    ).astype(jnp.bfloat16)
    flat = (length, cols, HEADS * HEAD_DIM)
    return (grad_query.reshape(flat), grad_key.reshape(flat), grad_value.reshape(flat))


def body(tokens, conv_weight, gain, bands, w_query, w_key, w_value, w_out, grad_out):
    depth_dev, height_dev, width_win, width = tokens.shape
    columns = height_dev * width_win
    taps = conv_weight.astype(jnp.float32)
    side_pad = ((0, 0), (0, 0), (1, 1), (0, 0))
    rimmed = padded_2(tokens, (("grp", 0), ("inner", 1)), 1)
    filtered = (tokens.astype(jnp.float32) + conv_forward(jnp.pad(rimmed, side_pad), taps)).astype(
        jnp.bfloat16
    )
    normed = layer_norm(filtered, gain).astype(jnp.bfloat16)
    flat_normed = normed.reshape(depth_dev, columns, width)
    w_joint = jnp.concatenate([w_query, w_key, w_value], 1)
    joint = jnp.dot(flat_normed, w_joint, preferred_element_type=jnp.float32).astype(jnp.bfloat16)
    query_rows, key_rows, value_rows = (
        lax.all_to_all(joint[:, :, :width], "grp", split_axis=1, concat_axis=0, tiled=True),
        lax.all_to_all(
            joint[:, :, width : 2 * width], "grp", split_axis=1, concat_axis=0, tiled=True
        ),
        lax.all_to_all(joint[:, :, 2 * width :], "grp", split_axis=1, concat_axis=0, tiled=True),
    )
    attended_cols = attend(query_rows, key_rows, value_rows, bands)
    attended = lax.all_to_all(attended_cols, "grp", split_axis=0, concat_axis=1, tiled=True)
    filtered_flat = filtered.reshape(depth_dev, columns, width).astype(jnp.float32)
    output = (filtered_flat + jnp.dot(attended, w_out, preferred_element_type=jnp.float32)).astype(
        jnp.bfloat16
    )
    grad_flat = grad_out.reshape(depth_dev, columns, width)
    grad_att = jnp.dot(grad_flat, w_out.T, preferred_element_type=jnp.float32).astype(jnp.bfloat16)
    grad_att_cols = lax.all_to_all(grad_att, "grp", split_axis=1, concat_axis=0, tiled=True)
    grad_query, grad_key, grad_value = attend_back(
        query_rows, key_rows, value_rows, grad_att_cols, bands
    )
    back_query, back_key, back_value = (
        lax.all_to_all(grad_query, "grp", split_axis=0, concat_axis=1, tiled=True),
        lax.all_to_all(grad_key, "grp", split_axis=0, concat_axis=1, tiled=True),
        lax.all_to_all(grad_value, "grp", split_axis=0, concat_axis=1, tiled=True),
    )
    joined = jnp.concatenate([back_query, back_key, back_value], -1)
    grad_normed = jnp.dot(joined, w_joint.T, preferred_element_type=jnp.float32).astype(
        jnp.bfloat16
    )
    grad_normed = grad_normed.reshape(depth_dev, height_dev, width_win, width)
    grad_filtered = (
        grad_out.astype(jnp.float32) + layer_norm_back(filtered, gain, grad_normed)
    ).astype(jnp.bfloat16)
    grad_rimmed = padded_2(grad_filtered, (("grp", 0), ("inner", 1)), 1)
    grad_tokens = (
        grad_filtered.astype(jnp.float32) + conv_adjoint(jnp.pad(grad_rimmed, side_pad), taps)
    ).astype(jnp.bfloat16)
    return (output.reshape(depth_dev, height_dev, width_win, width), grad_tokens)


def solution(mesh):
    in_specs = (
        P("grp", "inner", None, None),
        P(),
        P(),
        P(),
        P(),
        P(),
        P(),
        P(),
        P("grp", "inner", None, None),
    )
    out_specs = (P("grp", "inner", None, None), P("grp", "inner", None, None))
    return jax.shard_map(body, mesh=mesh, in_specs=in_specs, out_specs=out_specs, check_vma=False)
```

profile of v0, /device:TPU:239, one launch (start us, length us, event | category | flops | bytes accessed | tf_op | source)
XLA Modules:
  0.0 201.7 jit_solution(1169694086122340193)
XLA Ops:
  1.5 4.4 %collective-permute-start = (bf16[1,4,8,512]{3,2,1,0:T(8,128)(2,1)S(1)}, bf16[1,4,8,512]{3,2,1,0:T(8,128)(2,1)S(1)}, u32[]{:S(2)}, u32[]{:S(2)}) collective-permute-start(bf16[1,4,8,512]{3,2,1,0:T(8,128)(2,1)S(1)} %get-tuple-element.18), channel_id=1, source_target_pairs={{0,32},{32,64},{64,96},{96,128},{128,160},{160,192},{192,224},{224... | collective-permute-start | bytes 98312 | tf_op jit(solution)/shard_map/ppermute | solution.py:20
  10.5 7.2 %all-to-all-start.4 = ((bf16[16,32,512]{2,0,1:T(8,128)(2,1)}), bf16[16,32,512]{2,0,1:T(8,128)(2,1)S(1)}, u32[]{:S(2)}, u32[]{:S(2)}) async-start(bf16[16,32,512]{2,0,1:T(8,128)(2,1)} %copy.95), calls=%async_computation.4 | async-start | bytes 1048576 | tf_op jit(solution)/shard_map/all_to_all | solution.py:177
  17.9 5.5 %collective-permute-start.2 = (bf16[18,1,8,512]{3,2,1,0:T(8,128)(2,1)S(1)}, bf16[18,1,8,512]{3,2,1,0:T(8,128)(2,1)S(1)}, u32[]{:S(2)}, u32[]{:S(2)}) collective-permute-start(bf16[18,1,8,512]{3,2,1,0:T(8,128)(2,1)S(1)} %get-tuple-element.13), channel_id=1, source_target_pairs={{0,1},{1,2},{2,3},{3,4},{4,5},{5,6},{6,7},{7,8},{8,9},{9,10},{10,1... | collective-permute-start | bytes 442376 | tf_op jit(solution)/shard_map/ppermute | solution.py:20
  28.6 3.5 %collective-permute-done.3 = bf16[18,1,8,512]{3,2,1,0:T(8,128)(2,1)S(1)} collective-permute-done((bf16[18,1,8,512]{3,2,1,0:T(8,128)(2,1)S(1)}, bf16[18,1,8,512]{3,2,1,0:T(8,128)(2,1)S(1)}, u32[]{:S(2)}, u32[]{:S(2)}) %collective-permute-start.3) | collective-permute-done | bytes 147488 | tf_op jit(solution)/shard_map/ppermute | solution.py:22
  33.1 4.2 %convert_reduce_fusion = (f32[16,4,8]{2,1,0:T(4,128)S(1)}, bf16[16,4,8,512]{3,2,1,0:T(8,128)(2,1)S(1)}) fusion(bf16[18,6,10,512]{3,2,1,0:T(8,128)(2,1)S(1)} %select_maximum_fusion.4, f32[512]{0:T(512)S(1)} %bitcast.200, bf16[18,1,8,512]{3,2,1,0:T(8,128)(2,1)S(1)} %collective-permute-done.3, bf16[18,4,8,512]{3,2,1,0:T(8,128)(2,1)S(1)} %constant_dynamic-update-slice_fusion, ...), kind=kLoop, calls=%fused_computation.35 | loop fusion | flops 24116736 | bytes 11493376 | tf_op jit(solution)/shard_map/reduce_sum | solution.py:63
  40.0 7.8 %all-to-all-start.1 = ((bf16[16,32,512]{2,0,1:T(8,128)(2,1)}), bf16[16,32,512]{2,0,1:T(8,128)(2,1)S(1)}, u32[]{:S(2)}, u32[]{:S(2)}) async-start(bf16[16,32,512]{2,0,1:T(8,128)(2,1)} %copy.84), calls=%async_computation.1 | async-start | bytes 1048576 | tf_op jit(solution)/shard_map/all_to_all | solution.py:163
  48.9 8.9 %all-to-all-done.1 = bf16[16,32,512]{2,0,1:T(8,128)(2,1)S(1)} async-done(((bf16[16,32,512]{2,0,1:T(8,128)(2,1)}), bf16[16,32,512]{2,0,1:T(8,128)(2,1)S(1)}, u32[]{:S(2)}, u32[]{:S(2)}) %all-to-all-start.1) | async-done | bytes 524320 | tf_op jit(solution)/shard_map/all_to_all | solution.py:163
  57.8 5.9 %all-to-all-start.2 = ((bf16[16,32,512]{2,0,1:T(8,128)(2,1)}), bf16[16,32,512]{2,0,1:T(8,128)(2,1)S(1)}, u32[]{:S(2)}, u32[]{:S(2)}) async-start(bf16[16,32,512]{2,0,1:T(8,128)(2,1)} %copy.86), calls=%async_computation.2 | async-start | bytes 1048576 | tf_op jit(solution)/shard_map/all_to_all | solution.py:164
  64.8 8.9 %all-to-all-done.2 = bf16[16,32,512]{2,0,1:T(8,128)(2,1)S(1)} async-done(((bf16[16,32,512]{2,0,1:T(8,128)(2,1)}), bf16[16,32,512]{2,0,1:T(8,128)(2,1)S(1)}, u32[]{:S(2)}, u32[]{:S(2)}) %all-to-all-start.2) | async-done | bytes 524320 | tf_op jit(solution)/shard_map/all_to_all | solution.py:164
  73.7 6.5 %all-to-all-start = ((bf16[16,32,512]{2,0,1:T(8,128)(2,1)}), bf16[16,32,512]{2,0,1:T(8,128)(2,1)}, u32[]{:S(2)}, u32[]{:S(2)}) async-start(bf16[16,32,512]{2,0,1:T(8,128)(2,1)} %copy.82), calls=%async_computation | async-start | bytes 1048576 | tf_op jit(solution)/shard_map/all_to_all | solution.py:167
  95.3 3.7 %fusion.114 = (f32[2,8,256]{2,1,0:T(8,128)S(1)}, f32[2,8,256,256]{2,3,1,0:T(8,128)}) fusion(pred[256,256]{0,1:T(8,128)(4,1)S(1)} %compare_and_fusion, bf16[256,2,8,64]{0,3,2,1:T(8,128)(2,1)S(1)} %copy-done.5, bf16[256,2,8,64]{0,3,2,1:T(8,128)(2,1)S(1)} %copy-done.6), kind=kOutput, calls=%fused_computation.167 | convolution fusion | flops 139460864 | bytes 5324800 | tf_op jit(solution)/shard_map/sub | solution.py:103
  99.1 8.0 %fusion.25 = bf16[2,8,64,256]{3,2,1,0:T(8,128)(2,1)} fusion(bf16[256,2,8,64]{0,3,2,1:T(8,128)(2,1)S(1)} %copy-done.6, f32[2,8,256,256]{2,3,1,0:T(8,128)} %fusion.115, f32[2,8,256,256]{2,3,1,0:T(8,128)} %get-tuple-element.49, f32[2,8,256]{2,1,0:T(8,128)S(1)} %get-tuple-element.48), kind=kOutput, calls=%fused_computation.44 | convolution fusion | flops 141824256 | bytes 9453568 | tf_op jit(solution)/shard_map/chqk,kchd->qchd/dot_general | solution.py:139
  109.1 5.9 %all-to-all-start.5 = ((bf16[256,2,512]{2,1,0:T(2,128)(2,1)}), bf16[256,2,512]{2,1,0:T(2,128)(2,1)S(1)}, u32[]{:S(2)}, u32[]{:S(2)}) async-start(bf16[256,2,512]{2,1,0:T(2,128)(2,1)} %copy.101), calls=%async_computation.5 | async-start | bytes 1048576 | tf_op jit(solution)/shard_map/all_to_all | solution.py:182
  114.9 8.0 %fusion.28 = bf16[2,8,64,256]{3,2,1,0:T(8,128)(2,1)} fusion(bf16[256,2,8,64]{0,3,2,1:T(8,128)(2,1)S(1)} %copy-done.5, f32[2,8,256,256]{2,3,1,0:T(8,128)} %fusion.115, f32[2,8,256,256]{2,3,1,0:T(8,128)} %get-tuple-element.49, f32[2,8,256]{2,1,0:T(8,128)S(1)} %get-tuple-element.48), kind=kOutput, calls=%fused_computation.45 | convolution fusion | flops 141824256 | bytes 9453568 | tf_op jit(solution)/shard_map/chqk,qchd->kchd/dot_general | solution.py:142
  125.0 7.2 %all-to-all-start.6 = ((bf16[256,2,512]{2,1,0:T(2,128)(2,1)}), bf16[256,2,512]{2,1,0:T(2,128)(2,1)S(1)}, u32[]{:S(2)}, u32[]{:S(2)}) async-start(bf16[256,2,512]{2,1,0:T(2,128)(2,1)} %copy.106), calls=%async_computation.6 | async-start | bytes 1048576 | tf_op jit(solution)/shard_map/all_to_all | solution.py:183
  132.2 3.7 %convolution_convert_fusion.2 = bf16[2,8,64,256]{3,2,1,0:T(8,128)(2,1)} fusion(bf16[256,2,8,64]{0,3,2,1:T(8,128)(2,1)S(1)} %copy.97, f32[2,8,256,256]{2,3,1,0:T(8,128)} %get-tuple-element.49, f32[2,8,256]{2,1,0:T(8,128)S(1)} %get-tuple-element.48), kind=kOutput, calls=%fused_computation.48 | convolution fusion | flops 136577024 | bytes 5259264 | tf_op jit(solution)/shard_map/chqk,qchd->kchd/dot_general | solution.py:134
  138.0 4.2 %all-to-all-done.6 = bf16[256,2,512]{2,1,0:T(2,128)(2,1)S(1)} async-done(((bf16[256,2,512]{2,1,0:T(2,128)(2,1)}), bf16[256,2,512]{2,1,0:T(2,128)(2,1)S(1)}, u32[]{:S(2)}, u32[]{:S(2)}) %all-to-all-start.6) | async-done | bytes 524320 | tf_op jit(solution)/shard_map/all_to_all | solution.py:183
  142.2 5.9 %all-to-all-start.7 = ((bf16[256,2,512]{2,1,0:T(2,128)(2,1)}), bf16[256,2,512]{2,1,0:T(2,128)(2,1)S(1)}, u32[]{:S(2)}, u32[]{:S(2)}) async-start(bf16[256,2,512]{2,1,0:T(2,128)(2,1)} %copy.111), calls=%async_computation.7 | async-start | bytes 1048576 | tf_op jit(solution)/shard_map/all_to_all | solution.py:184
  158.1 5.9 %all-to-all-start.3 = ((bf16[256,2,512]{2,1,0:T(2,128)(2,1)}), bf16[256,2,512]{2,1,0:T(2,128)(2,1)S(1)}, u32[]{:S(2)}, u32[]{:S(2)}) async-start(bf16[256,2,512]{2,1,0:T(2,128)(2,1)} %copy.92), calls=%async_computation.3 | async-start | bytes 1048576 | tf_op jit(solution)/shard_map/all_to_all | solution.py:170
  169.5 4.8 %collective-permute-start.4 = (bf16[1,4,8,512]{3,2,1,0:T(8,128)(2,1)S(1)}, bf16[1,4,8,512]{3,2,1,0:T(8,128)(2,1)S(1)}, u32[]{:S(2)}, u32[]{:S(2)}) collective-permute-start(bf16[1,4,8,512]{3,2,1,0:T(8,128)(2,1)S(1)} %get-tuple-element.15), channel_id=1, source_target_pairs={{0,32},{32,64},{64,96},{96,128},{128,160},{160,192},{192,224},{224... | collective-permute-start | bytes 98312 | tf_op jit(solution)/shard_map/ppermute | solution.py:20
  177.1 6.1 %collective-permute-done.5 = bf16[1,4,8,512]{3,2,1,0:T(8,128)(2,1)S(1)} collective-permute-done((bf16[1,4,8,512]{3,2,1,0:T(8,128)(2,1)S(1)}, bf16[1,4,8,512]{3,2,1,0:T(8,128)(2,1)S(1)}, u32[]{:S(2)}, u32[]{:S(2)}) %collective-permute-start.5) | collective-permute-done | bytes 32800 | tf_op jit(solution)/shard_map/ppermute | solution.py:22
  183.2 4.9 %collective-permute-start.6 = (bf16[18,1,8,512]{3,2,1,0:T(8,128)(2,1)S(1)}, bf16[18,1,8,512]{3,2,1,0:T(8,128)(2,1)S(1)}, u32[]{:S(2)}, u32[]{:S(2)}) collective-permute-start(bf16[18,1,8,512]{3,2,1,0:T(8,128)(2,1)S(1)} %get-tuple-element.11), channel_id=1, source_target_pairs={{0,1},{1,2},{2,3},{3,4},{4,5},{5,6},{6,7},{7,8},{8,9},{9,10},{10,1... | collective-permute-start | bytes 442376 | tf_op jit(solution)/shard_map/ppermute | solution.py:20
  191.3 4.8 %collective-permute-done.7 = bf16[18,1,8,512]{3,2,1,0:T(8,128)(2,1)S(1)} collective-permute-done((bf16[18,1,8,512]{3,2,1,0:T(8,128)(2,1)S(1)}, bf16[18,1,8,512]{3,2,1,0:T(8,128)(2,1)S(1)}, u32[]{:S(2)}, u32[]{:S(2)}) %collective-permute-start.7) | collective-permute-done | bytes 147488 | tf_op jit(solution)/shard_map/ppermute | solution.py:22
  197.3 4.4 %fusion.82 = bf16[16,4,8,512]{3,2,1,0:T(8,128)(2,1)} fusion(bf16[16,4,8,512]{3,2,1,0:T(8,128)(2,1)S(1)} %fusion.46, bf16[18,6,10,512]{3,2,1,0:T(8,128)(2,1)S(1)} %select_maximum_fusion, bf16[18,5,8,512]{3,2,1,0:T(8,128)(2,1)S(1)} %get-tuple-element.10, bf16[1,4,8,512]{3,2,1,0:T(8,128)(2,1)S(1)} %collective-permute-done.4, ...), kind=kLoop, calls=%fused_computation.98 | loop fusion | flops 22020096 | bytes 13752320 | tf_op jit(solution)/shard_map/convert_element_type | solution.py:197
  (105 shorter events, 60.0 us)
Async XLA Ops:
  0.6 7.2 %copy-start = (bf16[512,512]{1,0:T(8,128)(2,1)S(1)}, bf16[512,512]{1,0:T(8,128)(2,1)}, u32[]{:S(2)}) copy-start(bf16[512,512]{1,0:T(8,128)(2,1)} %param.16) | copy-start | bytes 1572868
  0.6 17.1 %copy-start.1 = (bf16[16,4,8,512]{3,2,1,0:T(8,128)(2,1)S(1)}, bf16[16,4,8,512]{3,2,1,0:T(8,128)(2,1)}, u32[]{:S(2)}) copy-start(bf16[16,4,8,512]{3,2,1,0:T(8,128)(2,1)} %param.9) | copy-start | bytes 1572868
  0.7 17.1 %copy-start.7 = (bf16[27,512]{1,0:T(8,128)(2,1)S(1)}, bf16[27,512]{1,0:T(8,128)(2,1)}, u32[]{:S(2)}) copy-start(bf16[27,512]{1,0:T(8,128)(2,1)} %param.10) | copy-start | bytes 82948
  1.5 16.2 %collective-permute-start = (bf16[1,4,8,512]{3,2,1,0:T(8,128)(2,1)S(1)}, bf16[1,4,8,512]{3,2,1,0:T(8,128)(2,1)S(1)}, u32[]{:S(2)}, u32[]{:S(2)}) collective-permute-start(bf16[1,4,8,512]{3,2,1,0:T(8,128)(2,1)S(1)} %get-tuple-element.18), channel_id=1, source_target_pairs={{0,32},{32,64},{64,96},{96,128},{128,160},{160,192},{192,224},{224... | collective-permute-start | bytes 98312 | tf_op jit(solution)/shard_map/ppermute | solution.py:20
  5.9 11.9 %collective-permute-start.1 = (bf16[1,4,8,512]{3,2,1,0:T(8,128)(2,1)S(1)}, bf16[1,4,8,512]{3,2,1,0:T(8,128)(2,1)S(1)}, u32[]{:S(2)}, u32[]{:S(2)}) collective-permute-start(bf16[1,4,8,512]{3,2,1,0:T(8,128)(2,1)S(1)} %get-tuple-element.17), channel_id=1, source_target_pairs={{32,0},{64,32},{96,64},{128,96},{160,128},{192,160},{224,192},{256... | collective-permute-start | bytes 98312 | tf_op jit(solution)/shard_map/ppermute | solution.py:22
  10.5 29.6 %all-to-all-start.4 = ((bf16[16,32,512]{2,0,1:T(8,128)(2,1)}), bf16[16,32,512]{2,0,1:T(8,128)(2,1)S(1)}, u32[]{:S(2)}, u32[]{:S(2)}) async-start(bf16[16,32,512]{2,0,1:T(8,128)(2,1)} %copy.95), calls=%async_computation.4 | async-start | bytes 1048576 | tf_op jit(solution)/shard_map/all_to_all | solution.py:177
  17.9 10.8 %collective-permute-start.2 = (bf16[18,1,8,512]{3,2,1,0:T(8,128)(2,1)S(1)}, bf16[18,1,8,512]{3,2,1,0:T(8,128)(2,1)S(1)}, u32[]{:S(2)}, u32[]{:S(2)}) collective-permute-start(bf16[18,1,8,512]{3,2,1,0:T(8,128)(2,1)S(1)} %get-tuple-element.13), channel_id=1, source_target_pairs={{0,1},{1,2},{2,3},{3,4},{4,5},{5,6},{6,7},{7,8},{8,9},{9,10},{10,1... | collective-permute-start | bytes 442376 | tf_op jit(solution)/shard_map/ppermute | solution.py:20
  23.4 8.8 %collective-permute-start.3 = (bf16[18,1,8,512]{3,2,1,0:T(8,128)(2,1)S(1)}, bf16[18,1,8,512]{3,2,1,0:T(8,128)(2,1)S(1)}, u32[]{:S(2)}, u32[]{:S(2)}) collective-permute-start(bf16[18,1,8,512]{3,2,1,0:T(8,128)(2,1)S(1)} %get-tuple-element.14), channel_id=1, source_target_pairs={{1,0},{2,1},{3,2},{4,3},{5,4},{6,5},{7,6},{8,7},{9,8},{10,9},{11,1... | collective-permute-start | bytes 442376 | tf_op jit(solution)/shard_map/ppermute | solution.py:22
  33.0 4.6 %copy-start.8 = (f32[512]{0:T(512)S(1)}, f32[512]{0:T(512)}, u32[]{:S(2)}) copy-start(f32[512]{0:T(512)} %param.11) | copy-start | bytes 6148
  33.0 4.6 %copy-start.10 = (bf16[512,512]{1,0:T(8,128)(2,1)S(1)}, bf16[512,512]{1,0:T(8,128)(2,1)}, u32[]{:S(2)}) copy-start(bf16[512,512]{1,0:T(8,128)(2,1)} %param.15) | copy-start | bytes 1572868
  38.7 24.9 %copy-start.9 = (s32[4,2]{0,1:T(2,128)S(1)}, s32[4,2]{0,1:T(2,128)}, u32[]{:S(2)}) copy-start(s32[4,2]{0,1:T(2,128)} %param.12) | copy-start | bytes 100
  40.0 17.8 %all-to-all-start.1 = ((bf16[16,32,512]{2,0,1:T(8,128)(2,1)}), bf16[16,32,512]{2,0,1:T(8,128)(2,1)S(1)}, u32[]{:S(2)}, u32[]{:S(2)}) async-start(bf16[16,32,512]{2,0,1:T(8,128)(2,1)} %copy.84), calls=%async_computation.1 | async-start | bytes 1048576 | tf_op jit(solution)/shard_map/all_to_all | solution.py:163
  57.8 22.6 %copy-start.3 = (bf16[16,32,512]{2,0,1:T(8,128)(2,1)}, bf16[16,32,512]{2,0,1:T(8,128)(2,1)S(1)}, u32[]{:S(2)}) copy-start(bf16[16,32,512]{2,0,1:T(8,128)(2,1)S(1)} %all-to-all-done.1) | copy-start | bytes 1572868
  57.8 15.9 %all-to-all-start.2 = ((bf16[16,32,512]{2,0,1:T(8,128)(2,1)}), bf16[16,32,512]{2,0,1:T(8,128)(2,1)S(1)}, u32[]{:S(2)}, u32[]{:S(2)}) async-start(bf16[16,32,512]{2,0,1:T(8,128)(2,1)} %copy.86), calls=%async_computation.2 | async-start | bytes 1048576 | tf_op jit(solution)/shard_map/all_to_all | solution.py:164
  73.7 6.8 %copy-start.4 = (bf16[16,32,512]{2,0,1:T(8,128)(2,1)}, bf16[16,32,512]{2,0,1:T(8,128)(2,1)S(1)}, u32[]{:S(2)}) copy-start(bf16[16,32,512]{2,0,1:T(8,128)(2,1)S(1)} %all-to-all-done.2) | copy-start | bytes 1572868
  73.7 16.6 %all-to-all-start = ((bf16[16,32,512]{2,0,1:T(8,128)(2,1)}), bf16[16,32,512]{2,0,1:T(8,128)(2,1)}, u32[]{:S(2)}, u32[]{:S(2)}) async-start(bf16[16,32,512]{2,0,1:T(8,128)(2,1)} %copy.82), calls=%async_computation | async-start | bytes 1048576 | tf_op jit(solution)/shard_map/all_to_all | solution.py:167
  109.1 15.9 %all-to-all-start.5 = ((bf16[256,2,512]{2,1,0:T(2,128)(2,1)}), bf16[256,2,512]{2,1,0:T(2,128)(2,1)S(1)}, u32[]{:S(2)}, u32[]{:S(2)}) async-start(bf16[256,2,512]{2,1,0:T(2,128)(2,1)} %copy.101), calls=%async_computation.5 | async-start | bytes 1048576 | tf_op jit(solution)/shard_map/all_to_all | solution.py:182
  125.0 17.2 %all-to-all-start.6 = ((bf16[256,2,512]{2,1,0:T(2,128)(2,1)}), bf16[256,2,512]{2,1,0:T(2,128)(2,1)S(1)}, u32[]{:S(2)}, u32[]{:S(2)}) async-start(bf16[256,2,512]{2,1,0:T(2,128)(2,1)} %copy.106), calls=%async_computation.6 | async-start | bytes 1048576 | tf_op jit(solution)/shard_map/all_to_all | solution.py:183
  142.2 15.9 %all-to-all-start.7 = ((bf16[256,2,512]{2,1,0:T(2,128)(2,1)}), bf16[256,2,512]{2,1,0:T(2,128)(2,1)S(1)}, u32[]{:S(2)}, u32[]{:S(2)}) async-start(bf16[256,2,512]{2,1,0:T(2,128)(2,1)} %copy.111), calls=%async_computation.7 | async-start | bytes 1048576 | tf_op jit(solution)/shard_map/all_to_all | solution.py:184
  158.1 18.2 %all-to-all-start.3 = ((bf16[256,2,512]{2,1,0:T(2,128)(2,1)}), bf16[256,2,512]{2,1,0:T(2,128)(2,1)S(1)}, u32[]{:S(2)}, u32[]{:S(2)}) async-start(bf16[256,2,512]{2,1,0:T(2,128)(2,1)} %copy.92), calls=%async_computation.3 | async-start | bytes 1048576 | tf_op jit(solution)/shard_map/all_to_all | solution.py:170
  169.5 7.6 %collective-permute-start.4 = (bf16[1,4,8,512]{3,2,1,0:T(8,128)(2,1)S(1)}, bf16[1,4,8,512]{3,2,1,0:T(8,128)(2,1)S(1)}, u32[]{:S(2)}, u32[]{:S(2)}) collective-permute-start(bf16[1,4,8,512]{3,2,1,0:T(8,128)(2,1)S(1)} %get-tuple-element.15), channel_id=1, source_target_pairs={{0,32},{32,64},{64,96},{96,128},{128,160},{160,192},{192,224},{224... | collective-permute-start | bytes 98312 | tf_op jit(solution)/shard_map/ppermute | solution.py:20
  174.3 8.8 %collective-permute-start.5 = (bf16[1,4,8,512]{3,2,1,0:T(8,128)(2,1)S(1)}, bf16[1,4,8,512]{3,2,1,0:T(8,128)(2,1)S(1)}, u32[]{:S(2)}, u32[]{:S(2)}) collective-permute-start(bf16[1,4,8,512]{3,2,1,0:T(8,128)(2,1)S(1)} %get-tuple-element.16), channel_id=1, source_target_pairs={{32,0},{64,32},{96,64},{128,96},{160,128},{192,160},{224,192},{256... | collective-permute-start | bytes 98312 | tf_op jit(solution)/shard_map/ppermute | solution.py:22
  183.2 8.1 %collective-permute-start.6 = (bf16[18,1,8,512]{3,2,1,0:T(8,128)(2,1)S(1)}, bf16[18,1,8,512]{3,2,1,0:T(8,128)(2,1)S(1)}, u32[]{:S(2)}, u32[]{:S(2)}) collective-permute-start(bf16[18,1,8,512]{3,2,1,0:T(8,128)(2,1)S(1)} %get-tuple-element.11), channel_id=1, source_target_pairs={{0,1},{1,2},{2,3},{3,4},{4,5},{5,6},{6,7},{7,8},{8,9},{9,10},{10,1... | collective-permute-start | bytes 442376 | tf_op jit(solution)/shard_map/ppermute | solution.py:20
  188.1 8.0 %collective-permute-start.7 = (bf16[18,1,8,512]{3,2,1,0:T(8,128)(2,1)S(1)}, bf16[18,1,8,512]{3,2,1,0:T(8,128)(2,1)S(1)}, u32[]{:S(2)}, u32[]{:S(2)}) collective-permute-start(bf16[18,1,8,512]{3,2,1,0:T(8,128)(2,1)S(1)} %get-tuple-element.12), channel_id=1, source_target_pairs={{1,0},{2,1},{3,2},{4,3},{5,4},{6,5},{7,6},{8,7},{9,8},{10,9},{11,1... | collective-permute-start | bytes 442376 | tf_op jit(solution)/shard_map/ppermute | solution.py:22
  (5 other events, 18.2 us)
where the time goes:
time: 203 us; the launch traced here: 202 us
  starting transfers between devices  79.6 us (39%)
  waiting for transfers between devices  43.9 us (22%)
  matrix products  36.5 us (18%)
  local copies, waits for them, and re-layouts  28.7 us (14%)
  other arithmetic  11.9 us (6%)
    ppermute x4, starting transfers between devices, padded_2(): lax.ppermute(tail, axis, [(i, (i + 1) % count) for i in range(ends)])  19.7 us
    ppermute x4, waiting for transfers between devices, padded_2(): lax.ppermute(head, axis, [((i + 1) % count, i) for i in range(ends)])  14.5 us
    all_to_all x1, waiting for transfers between devices, body(): lax.all_to_all(joint[:, :, width:2 * width], 'grp', split_axis=1, concat_...  8.92 us
    all_to_all x1, waiting for transfers between devices, body(): lax.all_to_all(joint[:, :, :width], 'grp', split_axis=1, concat_axis=0, t...  8.91 us
    dot_general x1, matrix products, attend_back(): jnp.einsum('chqk,qchd->kchd', grad_scores, query_heads, preferred_element...  7.99 us
    dot_general x1, matrix products, attend_back(): jnp.einsum('chqk,kchd->qchd', grad_scores, key_heads, preferred_element_t...  7.98 us
    all_to_all x1, starting transfers between devices, body(): lax.all_to_all(joint[:, :, :width], 'grp', split_axis=1, concat_axis=0, t...  7.77 us
    ppermute x4, starting transfers between devices, padded_2(): lax.ppermute(head, axis, [((i + 1) % count, i) for i in range(ends)])  7.68 us
  transfers between devices with their start and end apart: 16, of which 9 were waited for; matrix products, arithmetic and copies ran while one was open for 24% of the time, Pallas kernels for 0%

commit v1 on v0

v1 whole, which is shorter than its diff:
```python
import jax
import jax.numpy as jnp
from jax import lax
from jax.experimental import pallas as pl
from jax.experimental.pallas import tpu as pltpu
from jax.sharding import PartitionSpec as P

MESH = pl.DeviceIdType.MESH
F32 = jnp.float32
BF16 = jnp.bfloat16
WID = 512
DEP = 16
HGT = 4
WIN = 8
TOK = DEP * HGT * WIN
COLS = HGT * WIN
LEN = 256
PER = 2


def dot_nn(a, b):
    return lax.dot_general(a, b, (((1,), (0,)), ((), ())), preferred_element_type=F32)


def dot_nt(a, b):
    return lax.dot_general(a, b, (((1,), (1,)), ((), ())), preferred_element_type=F32)


def iota(shape, dim):
    return lax.broadcasted_iota(jnp.int32, shape, dim)


def conv_row(pad, taps, d, h, flip):
    acc = [None, None, None]
    for a in range(3):
        for b in range(3):
            v = pad[d + a, h + b]
            for c in range(3):
                tap = 9 * a + 3 * b + c
                term = taps[26 - tap if flip else tap] * v
                acc[c] = term if acc[c] is None else acc[c] + term
    row = iota((WIN, WID), 0)
    before = jnp.where(row == 0, 0.0, pltpu.roll(acc[0], 1, 0))
    after = jnp.where(row == WIN - 1, 0.0, pltpu.roll(acc[2], WIN - 1, 0))
    return acc[1] + before + after


def kernel(
    bands, conv_w, gain, tok_h, go_h, wq_h, wk_h, wv_h, wo_h, out_ref, gt_ref,
    tok, go, wq, wk, wv, wo, wkt, wvt, taps, pad, edge, rim_d, rim_h, rim_c,
    send_n, send_g, col_n, col_g, send_a, send_b, ret_a, ret_b,
    perm, perm_t, eye, bias, filt, normed, unit, scale,
    q_s, k_s, v_s, g_s, kt_s, vt_s, at_s, qt_s, gk_s, gv_s,
    load_sem, halo_ss, halo_rs, a2a_ss, a2a_rs,
):
    g = lax.axis_index("grp")
    i = lax.axis_index("inner")
    ng = lax.axis_size("grp")
    ni = lax.axis_size("inner")
    up_g, dn_g = lax.rem(g + 1, ng), lax.rem(g + ng - 1, ng)
    up_i, dn_i = lax.rem(i + 1, ni), lax.rem(i + ni - 1, ni)

    loads = []
    for n, (src, dst) in enumerate(
        ((tok_h, tok), (go_h, go), (wq_h, wq), (wk_h, wk), (wv_h, wv), (wo_h, wo))
    ):
        cp = pltpu.make_async_copy(src, dst, load_sem.at[n])
        cp.start()
        loads.append(cp)

    barrier = pltpu.get_barrier_semaphore()
    sides = ((g, up_i), (g, dn_i), (up_g, up_i), (up_g, dn_i), (dn_g, up_i), (dn_g, dn_i))

    def greet(step, carry):
        pl.semaphore_signal(
            barrier, inc=1, device_id=(lax.rem(g + step, ng), i), device_id_type=MESH
        )
        return carry

    lax.fori_loop(1, ng, greet, 0)
    for peer in sides:
        pl.semaphore_signal(barrier, inc=1, device_id=peer, device_id_type=MESH)

    conv_f = conv_w[...].astype(F32)
    for n in range(27):
        taps[n] = jnp.broadcast_to(conv_f[n : n + 1], (WIN, WID))

    loads[0].wait()

    def fill(d, carry):
        pad[1 + d, 1 : 1 + HGT] = (
            tok[pl.ds(d * COLS, COLS)].astype(F32).reshape(HGT, WIN, WID)
        )
        return carry

    def stage(phase):
        for n, h in enumerate((1, HGT)):
            edge[phase, n] = pad[1 : 1 + DEP, h].reshape(DEP * WIN, WID).astype(BF16)

    def halo_copies(phase, body):
        last = DEP * WIN - 16
        plan = (
            (body.at[pl.ds(TOK - COLS, COLS)], rim_d.at[phase, 0], (up_g, i)),
            (body.at[pl.ds(0, COLS)], rim_d.at[phase, 1], (dn_g, i)),
            (edge.at[phase, 1], rim_h.at[phase, 0], (g, up_i)),
            (edge.at[phase, 0], rim_h.at[phase, 1], (g, dn_i)),
            (edge.at[phase, 1, pl.ds(last, 16)], rim_c.at[phase, 0], (up_g, up_i)),
            (edge.at[phase, 1, pl.ds(0, 16)], rim_c.at[phase, 1], (dn_g, up_i)),
            (edge.at[phase, 0, pl.ds(last, 16)], rim_c.at[phase, 2], (up_g, dn_i)),
            (edge.at[phase, 0, pl.ds(0, 16)], rim_c.at[phase, 3], (dn_g, dn_i)),
        )
        return [
            pltpu.make_async_remote_copy(
                src_ref=src, dst_ref=dst, send_sem=halo_ss.at[phase, n],
                recv_sem=halo_rs.at[phase, n], device_id=dev, device_id_type=MESH,
            )
            for n, (src, dst, dev) in enumerate(plan)
        ]

    def rim_in(phase):
        lo_g, hi_g = g > 0, g < ng - 1
        lo_i, hi_i = i > 0, i < ni - 1

        def part(ok, val):
            return jnp.where(ok, val.astype(F32), 0.0)

        pad[0, 1 : 1 + HGT] = part(lo_g, rim_d[phase, 0]).reshape(HGT, WIN, WID)
        pad[DEP + 1, 1 : 1 + HGT] = part(hi_g, rim_d[phase, 1]).reshape(HGT, WIN, WID)
        pad[1 : 1 + DEP, 0] = part(lo_i, rim_h[phase, 0]).reshape(DEP, WIN, WID)
        pad[1 : 1 + DEP, HGT + 1] = part(hi_i, rim_h[phase, 1]).reshape(DEP, WIN, WID)
        pad[0, 0] = part(lo_g & lo_i, rim_c[phase, 0])[WIN:]
        pad[DEP + 1, 0] = part(hi_g & lo_i, rim_c[phase, 1])[:WIN]
        pad[0, HGT + 1] = part(lo_g & hi_i, rim_c[phase, 2])[WIN:]
        pad[DEP + 1, HGT + 1] = part(hi_g & hi_i, rim_c[phase, 3])[:WIN]

    def own_rows(owner):
        return pl.ds(pl.multiple_of(owner * DEP, DEP), DEP)

    def exchange(kind, col, src, dst):
        def one(step, carry):
            p = lax.rem(g + step, ng)
            pltpu.make_async_remote_copy(
                src_ref=src.at[col, own_rows(p)], dst_ref=dst.at[col, own_rows(g)],
                send_sem=a2a_ss.at[kind, col], recv_sem=a2a_rs.at[kind, col],
                device_id=(p, i), device_id_type=MESH,
            ).start()
            return carry

        lax.fori_loop(1, ng, one, 0)
        pltpu.make_async_copy(
            src.at[col, own_rows(g)], dst.at[col, own_rows(g)], a2a_rs.at[kind, col]
        ).start()

    def arrived(kind, col, dst):
        pltpu.make_async_copy(dst.at[col], dst.at[col], a2a_rs.at[kind, col]).wait()

    def sent(kind, col, src):
        rows = pl.ds(0, LEN - DEP)
        pltpu.make_async_copy(
            src.at[col, rows], src.at[col, rows], a2a_ss.at[kind, col]
        ).wait()

    lax.fori_loop(0, DEP, fill, 0)
    stage(0)
    pl.semaphore_wait(barrier, ng - 1 + len(sides))
    halos = halo_copies(0, tok)
    for cp in halos:
        cp.start()

    shape = (TOK, TOK)

    def token_of(s):
        return (s & 15) * COLS + ((s >> 4) & 15) * PER + (s >> 8)

    perm[...] = jnp.where(iota(shape, 1) == token_of(iota(shape, 0)), 1.0, 0.0).astype(BF16)
    perm_t[...] = jnp.where(iota(shape, 0) == token_of(iota(shape, 1)), 1.0, 0.0).astype(BF16)
    eye[...] = jnp.where(iota(shape, 0) == iota(shape, 1), 1.0, 0.0).astype(BF16)

    loads[1].wait()
    for col in range(PER):
        send_g[col] = dot_nn(perm[col * LEN : (col + 1) * LEN], go[...]).astype(BF16)
        exchange(0, col, send_g, col_g)

    for cp in loads[2:]:
        cp.wait()
    wkt[...] = dot_nt(eye[...], wk[...]).astype(BF16)
    wvt[...] = dot_nt(eye[...], wv[...]).astype(BF16)

    square = (LEN, LEN)
    key_block = iota(square, 0) >> 6
    query_block = iota(square, 1) >> 6
    lower = jnp.zeros(square, jnp.int32)
    upper = jnp.zeros(square, jnp.int32)
    for n in range(4):
        lower = jnp.where(query_block == n, bands[n, 0], lower)
        upper = jnp.where(query_block == n, bands[n, 1], upper)
    allowed = (key_block >= query_block - lower) & (key_block <= query_block + upper)
    bias[...] = jnp.where(allowed, 0.0, -1e30)

    for cp in halos:
        cp.wait()
    rim_in(0)

    gain_row = gain[...]

    def forward(d, carry):
        rows = pl.ds(pl.multiple_of(d * COLS, COLS), COLS)
        conv = [
            conv_row(pad, taps, d, h, False) + pad[d + 1, h + 1] for h in range(HGT)
        ]
        vals = jnp.concatenate(conv, 0).astype(BF16)
        filt[rows] = vals
        vals = vals.astype(F32)
        centred = vals - jnp.sum(vals, -1, keepdims=True) * (1.0 / WID)
        var = jnp.sum(centred * centred, -1, keepdims=True) * (1.0 / WID)
        inv = lax.rsqrt(var + 1e-05)
        xhat = centred * inv
        unit[rows] = xhat
        scale[rows] = jnp.broadcast_to(inv, (COLS, 128))
        normed[rows] = (xhat * gain_row).astype(BF16)
        return carry

    lax.fori_loop(0, DEP, forward, 0)
    for col in range(PER):
        send_n[col] = dot_nn(perm[col * LEN : (col + 1) * LEN], normed[...]).astype(BF16)
        exchange(1, col, send_n, col_n)

    low_half = iota((LEN, 128), 1) < 64

    def halves(x):
        zero = jnp.zeros_like(x)
        return jnp.where(low_half, x, zero), jnp.where(low_half, zero, x)

    for col in range(PER):
        arrived(0, col, col_g)
        g_s[...] = dot_nt(col_g[col], wo[...]).astype(BF16)
        arrived(1, col, col_n)
        x = col_n[col]
        q_s[...] = (dot_nn(x, wq[...]).astype(BF16).astype(F32) * 0.125).astype(BF16)
        k_s[...] = dot_nn(x, wk[...]).astype(BF16)
        v_s[...] = dot_nn(x, wv[...]).astype(BF16)
        kt_s[...] = dot_nt(wkt[...], x).astype(BF16)
        vt_s[...] = dot_nt(wvt[...], x).astype(BF16)

        def heads(pair, carry):
            lanes = pl.ds(pl.multiple_of(pair * 128, 128), 128)
            q2, g2 = q_s[:, lanes], g_s[:, lanes]
            ks, vs = halves(k_s[:, lanes]), halves(v_s[:, lanes])
            qs, gs = halves(q2), halves(g2)
            gk = None
            gv = None
            for n in range(2):
                feats = pl.ds(pl.multiple_of(pair * 128 + n * 64, 64), 64)
                scores = dot_nt(ks[n], q2) + bias[...]
                expo = jnp.exp(scores - jnp.max(scores, 0, keepdims=True))
                probs = expo * (1.0 / jnp.sum(expo, 0, keepdims=True))
                weights = probs.astype(BF16)
                at_s[feats] = dot_nn(vt_s[feats], weights).astype(BF16)
                grad_p = dot_nt(vs[n], g2)
                centre = jnp.sum(probs * grad_p, 0, keepdims=True)
                grad_s = (probs * (grad_p - centre)).astype(BF16)
                qt_s[feats] = (dot_nn(kt_s[feats], grad_s) * 0.125).astype(BF16)
                part_v = dot_nn(weights, gs[n])
                part_k = dot_nn(grad_s, qs[n])
                gv = part_v if gv is None else gv + part_v
                gk = part_k if gk is None else gk + part_k
            gk_s[:, lanes] = gk.astype(BF16)
            gv_s[:, lanes] = gv.astype(BF16)
            return carry

        lax.fori_loop(0, 4, heads, 0)
        small = eye[0:LEN, 0:LEN]
        gq = dot_nt(small, qt_s[...]).astype(BF16)
        send_b[col] = (
            dot_nt(gq, wq[...]) + dot_nt(gk_s[...], wk[...]) + dot_nt(gv_s[...], wv[...])
        ).astype(BF16)
        exchange(2, col, send_b, ret_b)
        send_a[col] = dot_nt(small, at_s[...]).astype(BF16)
        exchange(3, col, send_a, ret_a)

    for col in range(PER):
        arrived(2, col, ret_b)

    normed_grad = [dot_nn(perm_t[:, 0:LEN], ret_b[0]), dot_nn(perm_t[:, LEN:TOK], ret_b[1])]
    unit_grad = (normed_grad[0] + normed_grad[1]) * gain_row
    xhat = unit[...]
    mean = jnp.sum(unit_grad, -1, keepdims=True) * (1.0 / WID)
    along = jnp.sum(unit_grad * xhat, -1, keepdims=True) * (1.0 / WID)
    inv = scale[...][:, 0:1]
    grad_f = (go[...].astype(F32) + inv * (unit_grad - mean - xhat * along)).astype(BF16)
    tok[...] = grad_f

    lax.fori_loop(0, DEP, fill, 0)
    stage(1)
    halos = halo_copies(1, tok)
    for cp in halos:
        cp.start()

    for col in range(PER):
        arrived(3, col, ret_a)
    att = (
        dot_nn(perm_t[:, 0:LEN], ret_a[0]) + dot_nn(perm_t[:, LEN:TOK], ret_a[1])
    ).astype(BF16)
    out_ref[...] = (filt[...].astype(F32) + dot_nn(att, wo[...])).astype(BF16)

    for cp in halos:
        cp.wait()
    rim_in(1)

    def adjoint(d, carry):
        rows = pl.ds(pl.multiple_of(d * COLS, COLS), COLS)
        conv = [conv_row(pad, taps, d, h, True) + pad[d + 1, h + 1] for h in range(HGT)]
        gt_ref[rows] = jnp.concatenate(conv, 0).astype(BF16)
        return carry

    lax.fori_loop(0, DEP, adjoint, 0)
    for kind, src in enumerate((send_g, send_n, send_b, send_a)):
        for col in range(PER):
            sent(kind, col, src)


def body(tokens, conv_weight, gain, bands, w_query, w_key, w_value, w_out, grad_out):
    whole = (TOK, WID)
    pair = (PER, LEN, WID)
    vmem = pl.BlockSpec(memory_space=pltpu.VMEM)
    hbm = pl.BlockSpec(memory_space=pltpu.HBM)
    scratch = [
        pltpu.VMEM(whole, BF16), pltpu.VMEM(whole, BF16),
        *[pltpu.VMEM((WID, WID), BF16) for _ in range(6)],
        pltpu.VMEM((27, WIN, WID), F32),
        pltpu.VMEM((DEP + 2, HGT + 2, WIN, WID), F32),
        pltpu.VMEM((2, 2, DEP * WIN, WID), BF16),
        pltpu.VMEM((2, 2, COLS, WID), BF16),
        pltpu.VMEM((2, 2, DEP * WIN, WID), BF16),
        pltpu.VMEM((2, 4, 16, WID), BF16),
        *[pltpu.VMEM(pair, BF16) for _ in range(8)],
        *[pltpu.VMEM((TOK, TOK), BF16) for _ in range(3)],
        pltpu.VMEM((LEN, LEN), F32),
        pltpu.VMEM(whole, BF16), pltpu.VMEM(whole, BF16),
        pltpu.VMEM(whole, F32),
        pltpu.VMEM((TOK, 128), F32),
        *[pltpu.VMEM((LEN, WID), BF16) for _ in range(4)],
        *[pltpu.VMEM((WID, LEN), BF16) for _ in range(4)],
        *[pltpu.VMEM((LEN, WID), BF16) for _ in range(2)],
        pltpu.SemaphoreType.DMA((6,)),
        pltpu.SemaphoreType.DMA((2, 8)), pltpu.SemaphoreType.DMA((2, 8)),
        pltpu.SemaphoreType.DMA((4, PER)), pltpu.SemaphoreType.DMA((4, PER)),
    ]
    out, grad = pl.pallas_call(
        kernel,
        out_shape=(jax.ShapeDtypeStruct(whole, BF16), jax.ShapeDtypeStruct(whole, BF16)),
        in_specs=[pl.BlockSpec(memory_space=pltpu.SMEM), vmem, vmem] + [hbm] * 6,
        out_specs=(vmem, vmem),
        scratch_shapes=scratch,
        compiler_params=pltpu.CompilerParams(
            collective_id=0, has_side_effects=True, vmem_limit_bytes=48 * 2**20
        ),
        name="sublayer",
    )(
        bands, conv_weight, gain.reshape(1, WID), tokens.reshape(whole),
        grad_out.reshape(whole), w_query, w_key, w_value, w_out,
    )
    return out.reshape(tokens.shape), grad.reshape(tokens.shape)


def solution(mesh):
    slab = P("grp", "inner", None, None)
    in_specs = (slab, P(), P(), P(), P(), P(), P(), P(), slab)
    return jax.shard_map(
        body, mesh=mesh, in_specs=in_specs, out_specs=(slab, slab), check_vma=False
    )
```

time: 203 us -> 83.6 us (0.41)
  the two profiles are of different devices: /device:TPU:239 before, /device:TPU:1 now
where the time goes in v1:
time: 83.6 us; the launch traced here: 82.6 us
  Pallas kernels  72.6 us (87%)
  local copies, waits for them, and re-layouts  9.35 us (11%)
    pallas_call x1, Pallas kernels, body(): pl.pallas_call(kernel, out_shape=(jax.ShapeDtypeStruct(whole, BF16), jax....  72.6 us
    unnamed x21, local copies, waits for them, and re-layouts  9.35 us

profile of v1, /device:TPU:1, one launch (start us, length us, event | category | flops | bytes accessed | tf_op | source)
XLA Modules:
  0.0 82.6 jit_solution(17441402389904172315)
XLA Ops:
  0.6 0.0 copy-start.8
  0.6 0.0 copy-start.7
  0.6 0.7 copy-done.8
  1.3 0.1 copy.11.bands
  1.4 0.0 copy-done.7
  1.4 0.0 copy-start
  1.4 1.0 %copy-done = bf16[16,4,8,512]{3,2,1,0:T(8,128)(2,1)S(1)} copy-done((bf16[16,4,8,512]{3,2,1,0:T(8,128)(2,1)S(1)}, bf16[16,4,8,512]{3,2,1,0:T(8,128)(2,1)}, u32[]{:S(2)}) %copy-start) | copy-done | bytes 524312
  2.4 0.0 copy-start.1
  2.5 1.0 %copy-done.1 = bf16[16,4,8,512]{3,2,1,0:T(8,128)(2,1)S(1)} copy-done((bf16[16,4,8,512]{3,2,1,0:T(8,128)(2,1)S(1)}, bf16[16,4,8,512]{3,2,1,0:T(8,128)(2,1)}, u32[]{:S(2)}) %copy-start.1) | copy-done | bytes 524312
  3.5 0.0 copy-start.2
  3.5 1.0 %copy-done.2 = bf16[512,512]{1,0:T(8,128)(2,1)S(1)} copy-done((bf16[512,512]{1,0:T(8,128)(2,1)S(1)}, bf16[512,512]{1,0:T(8,128)(2,1)}, u32[]{:S(2)}) %copy-start.2) | copy-done | bytes 524312
  4.5 0.0 copy-start.3
  4.5 1.0 %copy-done.3 = bf16[512,512]{1,0:T(8,128)(2,1)S(1)} copy-done((bf16[512,512]{1,0:T(8,128)(2,1)S(1)}, bf16[512,512]{1,0:T(8,128)(2,1)}, u32[]{:S(2)}) %copy-start.3) | copy-done | bytes 524312
  5.6 0.0 copy-start.4
  5.6 1.0 %copy-done.4 = bf16[512,512]{1,0:T(8,128)(2,1)S(1)} copy-done((bf16[512,512]{1,0:T(8,128)(2,1)S(1)}, bf16[512,512]{1,0:T(8,128)(2,1)}, u32[]{:S(2)}) %copy-start.4) | copy-done | bytes 524312
  6.6 0.0 copy-start.5
  6.6 1.0 %copy-done.5 = bf16[512,512]{1,0:T(8,128)(2,1)S(1)} copy-done((bf16[512,512]{1,0:T(8,128)(2,1)S(1)}, bf16[512,512]{1,0:T(8,128)(2,1)}, u32[]{:S(2)}) %copy-start.5) | copy-done | bytes 524312
  7.7 0.0 copy-start.6
  7.7 0.8 copy-done.6
  8.4 72.6 %sublayer.1 = (bf16[512,512]{1,0:T(8,128)(2,1)S(1)}, bf16[512,512]{1,0:T(8,128)(2,1)S(1)}) custom-call(s32[4,2]{1,0:T(4,128)S(1)} %copy.11.bands, bf16[27,512]{1,0:T(8,128)(2,1)S(1)} %copy-done.6, f32[1,512]{1,0:T(1,128)S(1)} %bitcast.9, bf16[512,512]{1,0:T(8,128)(2,1)S(1)} %bitcast.5, bf16[512,512]{1,0:T(8,128)(2,1)S(1)} %bitcast.6, ...), custom_call_target="tpu_custom_call" | custom-call | tf_op jit(solution)/shard_map/sublayer/pallas_call | solution.py:349
  81.0 0.8 copy.14
  81.8 0.8 copy.15
Async XLA Ops:
  0.6 0.7 copy-start.8
  0.6 0.8 copy-start.7
  1.4 1.0 %copy-start = (bf16[16,4,8,512]{3,2,1,0:T(8,128)(2,1)S(1)}, bf16[16,4,8,512]{3,2,1,0:T(8,128)(2,1)}, u32[]{:S(2)}) copy-start(bf16[16,4,8,512]{3,2,1,0:T(8,128)(2,1)} %param.9) | copy-start | bytes 1572868
  2.4 1.0 %copy-start.1 = (bf16[16,4,8,512]{3,2,1,0:T(8,128)(2,1)S(1)}, bf16[16,4,8,512]{3,2,1,0:T(8,128)(2,1)}, u32[]{:S(2)}) copy-start(bf16[16,4,8,512]{3,2,1,0:T(8,128)(2,1)} %param.17) | copy-start | bytes 1572868
  3.5 1.0 %copy-start.2 = (bf16[512,512]{1,0:T(8,128)(2,1)S(1)}, bf16[512,512]{1,0:T(8,128)(2,1)}, u32[]{:S(2)}) copy-start(bf16[512,512]{1,0:T(8,128)(2,1)} %wq_h.1) | copy-start | bytes 1572868
  4.5 1.0 %copy-start.3 = (bf16[512,512]{1,0:T(8,128)(2,1)S(1)}, bf16[512,512]{1,0:T(8,128)(2,1)}, u32[]{:S(2)}) copy-start(bf16[512,512]{1,0:T(8,128)(2,1)} %wk_h.1) | copy-start | bytes 1572868
  5.6 1.0 %copy-start.4 = (bf16[512,512]{1,0:T(8,128)(2,1)S(1)}, bf16[512,512]{1,0:T(8,128)(2,1)}, u32[]{:S(2)}) copy-start(bf16[512,512]{1,0:T(8,128)(2,1)} %wv_h.1) | copy-start | bytes 1572868
  6.6 1.0 %copy-start.5 = (bf16[512,512]{1,0:T(8,128)(2,1)S(1)}, bf16[512,512]{1,0:T(8,128)(2,1)}, u32[]{:S(2)}) copy-start(bf16[512,512]{1,0:T(8,128)(2,1)} %wo_h.1) | copy-start | bytes 1572868
  7.7 0.8 copy-start.6

commit v2 on v1

v2 whole, which is shorter than its diff:
```python
import jax
import jax.numpy as jnp
from jax import lax
from jax.experimental import pallas as pl
from jax.experimental.pallas import tpu as pltpu
from jax.sharding import PartitionSpec as P

MESH = pl.DeviceIdType.MESH
F32 = jnp.float32
BF16 = jnp.bfloat16
WID = 512
DEP = 16
HGT = 4
WIN = 8
TOK = DEP * HGT * WIN
COLS = HGT * WIN
LEN = 256
PER = 2


def dot_nn(a, b):
    return lax.dot_general(a, b, (((1,), (0,)), ((), ())), preferred_element_type=F32)


def dot_nt(a, b):
    return lax.dot_general(a, b, (((1,), (1,)), ((), ())), preferred_element_type=F32)


def iota(shape, dim):
    return lax.broadcasted_iota(jnp.int32, shape, dim)


def conv_row(pad, taps, d, h, flip):
    acc = [None, None, None]
    for a in range(3):
        for b in range(3):
            v = pad[d + a, h + b]
            for c in range(3):
                tap = 9 * a + 3 * b + c
                term = taps[26 - tap if flip else tap] * v
                acc[c] = term if acc[c] is None else acc[c] + term
    row = iota((WIN, WID), 0)
    before = jnp.where(row == 0, 0.0, pltpu.roll(acc[0], 1, 0))
    after = jnp.where(row == WIN - 1, 0.0, pltpu.roll(acc[2], WIN - 1, 0))
    return acc[1] + before + after


def kernel(
    bands_h, conv_h, gain_h, tok_h, go_h, wq_h, wk_h, wv_h, wo_h, out_h, grad_h,
    bands, conv_w, gain, tok, go, wq, wk, wv, wo, wqt, wkt, wvt, taps, pad, edge,
    rim_d, rim_h, rim_c, send_n, send_g, col_n, col_g, send_a, send_b, ret_a, ret_b,
    swap, eye, bias, hot, filt, normed, unit, scale, grad_f, out, gt,
    k_s, v_s, qt_s, kt_s, vt_s, gt_s, at_s, gq_s, gk_s, gv_s, exp_s, inv_s,
    load_sem, halo_ss, halo_rs, a2a_ss, a2a_rs, store_sem,
):
    g = lax.axis_index("grp")
    i = lax.axis_index("inner")
    ng = lax.axis_size("grp")
    ni = lax.axis_size("inner")
    up_g, dn_g = lax.rem(g + 1, ng), lax.rem(g + ng - 1, ng)
    up_i, dn_i = lax.rem(i + 1, ni), lax.rem(i + ni - 1, ni)

    pairs = (
        (tok_h, tok), (conv_h, conv_w), (go_h, go), (bands_h, bands), (gain_h, gain),
        (wq_h, wq), (wk_h, wk), (wv_h, wv), (wo_h, wo),
    )
    loads = [
        pltpu.make_async_copy(src, dst, load_sem.at[n]) for n, (src, dst) in enumerate(pairs)
    ]
    for cp in loads:
        cp.start()

    barrier = pltpu.get_barrier_semaphore()
    sides = ((g, up_i), (g, dn_i), (up_g, up_i), (up_g, dn_i), (dn_g, up_i), (dn_g, dn_i))

    def greet(step, carry):
        pl.semaphore_signal(
            barrier, inc=1, device_id=(lax.rem(g + step, ng), i), device_id_type=MESH
        )
        return carry

    for peer in sides:
        pl.semaphore_signal(barrier, inc=1, device_id=peer, device_id_type=MESH)
    lax.fori_loop(1, ng, greet, 0)

    last = DEP * WIN - 16

    def halo(phase, k, n, src, dst, dev):
        return pltpu.make_async_remote_copy(
            src_ref=src, dst_ref=dst, send_sem=halo_ss.at[phase, k, n],
            recv_sem=halo_rs.at[phase, k, n], device_id=dev, device_id_type=MESH,
        )

    def halo_depth(phase, body, k):
        return [
            halo(phase, k, 0, body.at[DEP - 1, k], rim_d.at[phase, 0, k], (up_g, i)),
            halo(phase, k, 1, body.at[0, k], rim_d.at[phase, 1, k], (dn_g, i)),
        ]

    def halo_side(phase, k):
        to = up_i if k else dn_i
        side = 1 - k
        return [
            halo(phase, k, 2, edge.at[phase, k], rim_h.at[phase, side], (g, to)),
            halo(
                phase, k, 3, edge.at[phase, k, pl.ds(last, 16)],
                rim_c.at[phase, 0, side], (up_g, to),
            ),
            halo(
                phase, k, 4, edge.at[phase, k, pl.ds(0, 16)],
                rim_c.at[phase, 1, side], (dn_g, to),
            ),
        ]

    def start(copies):
        for cp in copies:
            cp.start()

    def finish(copies):
        for cp in copies:
            cp.wait()

    in_g = (g > 0, g < ng - 1)
    in_i = (i > 0, i < ni - 1)

    def part(ok, val):
        return jnp.where(ok, val.astype(F32), 0.0)

    def rim_depth(phase, k):
        for n in range(2):
            pad[(DEP + 1) * n, 1 + 2 * k : 3 + 2 * k] = part(
                in_g[n], rim_d[phase, n, k]
            ).reshape(2, WIN, WID)

    def rim_side(phase, side):
        h = (HGT + 1) * side
        for n in range(2):
            corner = part(in_g[n] & in_i[side], rim_c[phase, n, side])
            pad[(DEP + 1) * n, h] = corner[:WIN] if n else corner[WIN:]
        pad[1 : 1 + DEP, h] = part(in_i[side], rim_h[phase, side]).reshape(DEP, WIN, WID)

    def own_rows(owner):
        return pl.ds(pl.multiple_of(owner * DEP, DEP), DEP)

    high, chip, core = lax.div(g, 8), lax.rem(lax.div(g, 2), 4), lax.rem(g, 2)
    peers = []
    for step in range(ng - 1):
        far_y, far_x = step < 8, (2, 1, 3, 0)[step // 2 % 4]
        same = 1 - (step + 1) % 2
        p_y = 1 - high if far_y else high
        p_x = lax.rem(chip + far_x, 4) if far_x else chip
        p_c = core if same else 1 - core
        peers.append(p_y * 8 + p_x * 2 + p_c)

    def exchange(kind, col, src, dst):
        for p in peers:
            pltpu.make_async_remote_copy(
                src_ref=src.at[col, own_rows(p)], dst_ref=dst.at[col, own_rows(g)],
                send_sem=a2a_ss.at[kind, col], recv_sem=a2a_rs.at[kind, col],
                device_id=(p, i), device_id_type=MESH,
            ).start()
        pltpu.make_async_copy(
            src.at[col, own_rows(g)], dst.at[col, own_rows(g)], a2a_rs.at[kind, col]
        ).start()

    def arrived(kind, col, dst):
        pltpu.make_async_copy(dst.at[col], dst.at[col], a2a_rs.at[kind, col]).wait()

    def sent(kind, col, src):
        rows = pl.ds(0, LEN - DEP)
        pltpu.make_async_copy(
            src.at[col, rows], src.at[col, rows], a2a_ss.at[kind, col]
        ).wait()

    loads[0].wait()

    def fill(d, carry):
        pad[1 + d, 1 : 1 + HGT] = tok[d].reshape(COLS, WID).astype(F32).reshape(HGT, WIN, WID)
        return carry

    lax.fori_loop(0, DEP, fill, 0)
    for k in range(2):
        edge[0, k] = pad[1 : 1 + DEP, 1 + 3 * k].reshape(DEP * WIN, WID).astype(BF16)
    pl.semaphore_wait(barrier, ng - 1 + len(sides))
    depth = halo_depth(0, tok, 0) + halo_depth(0, tok, 1)
    low, top = halo_side(0, 1), halo_side(0, 0)
    start(depth + low + top)

    square = (LEN, LEN)
    row, lane = iota(square, 0), iota(square, 1)
    swap[...] = jnp.where(lane == (row & 15) * 16 + (row >> 4), 1.0, 0.0).astype(BF16)
    eye[...] = jnp.where(row == lane, 1.0, 0.0).astype(BF16)

    loads[2].wait()
    for k in range(2):
        send_g[k] = dot_nn(swap[...], go[:, k].reshape(LEN, WID)).astype(BF16)
    exchange(0, 0, send_g, col_g)

    loads[1].wait()
    conv_f = conv_w[...].astype(F32)
    for n in range(27):
        taps[n] = jnp.broadcast_to(conv_f[n : n + 1], (WIN, WID))

    loads[3].wait()
    slim = (64, LEN)
    key_block = iota(slim, 0)
    query_block = iota(slim, 1) >> 6
    lower = jnp.zeros(slim, jnp.int32)
    upper = jnp.zeros(slim, jnp.int32)
    for n in range(4):
        lower = jnp.where(query_block == n, bands[0, n], lower)
        upper = jnp.where(query_block == n, bands[1, n], upper)
    banned = (key_block < query_block - lower) | (key_block > query_block + upper)
    bias[...] = jnp.where(banned & (key_block < 4), -1e30, 0.0).astype(BF16)
    wide = (LEN, 128)
    hot[...] = jnp.where((iota(wide, 1) & 63) == (iota(wide, 0) >> 6), 1.0, 0.0).astype(BF16)

    for cp in loads[4:]:
        cp.wait()
    gain_row = gain[...]

    finish(depth)
    for k in range(2):
        rim_depth(0, k)

    for k in range(2):
        finish(top if k else low)
        rim_side(0, k)

        def forward(d, carry, k=k):
            rows = pl.ds(pl.multiple_of(d * 16, 16), 16)
            conv = [
                conv_row(pad, taps, d, h, False) + pad[d + 1, h + 1]
                for h in (2 * k, 2 * k + 1)
            ]
            filt[k, rows] = jnp.concatenate(conv, 0).astype(BF16)
            return carry

        lax.fori_loop(0, DEP, forward, 0)
        for n in range(LEN // 64):
            rows = slice(n * 64, (n + 1) * 64)
            vals = filt[k, rows].astype(F32)
            centred = vals - jnp.sum(vals, -1, keepdims=True) * (1.0 / WID)
            var = jnp.sum(centred * centred, -1, keepdims=True) * (1.0 / WID)
            inv = lax.rsqrt(var + 1e-05)
            xhat = centred * inv
            unit[k, rows] = xhat
            scale[k, rows] = jnp.broadcast_to(inv, (64, 128))
            normed[k, rows] = (xhat * gain_row).astype(BF16)
        send_n[k] = dot_nn(swap[...], normed[k]).astype(BF16)
        exchange(1, k, send_n, col_n)

    exchange(0, 1, send_g, col_g)

    for src, dst in ((wq, wqt), (wk, wkt), (wv, wvt)):
        for n in range(2):
            half = slice(n * LEN, (n + 1) * LEN)
            dst[half] = dot_nt(eye[...], src[:, half]).astype(BF16)

    low_half = iota(wide, 1) < 64
    none = jnp.zeros(slim, BF16)
    ones = jnp.ones((16, LEN), BF16)

    def pair_of(pair, n):
        lanes = pl.ds(pair * 128, 128)
        feats = pl.ds(pair * 128 + n * 64, 64)
        return lanes, feats

    def attend(col):
        arrived(1, col, col_n)
        x = col_n[col]
        k_s[...] = dot_nn(x, wk[...]).astype(BF16)
        query = dot_nt(wqt[...], x).astype(BF16).astype(F32) * 0.125
        qt_s[col] = query.astype(BF16)
        vt_s[...] = dot_nt(wvt[...], x).astype(BF16)

        def heads(pair, carry):
            for n in range(2):
                lanes, feats = pair_of(pair, n)
                k2, qt = k_s[:, lanes], qt_s[col, feats]
                if n == 0:
                    keys = jnp.where(low_half, k2, hot[...])
                    queries = jnp.concatenate([qt, bias[...]], 0)
                else:
                    keys = jnp.where(low_half, hot[...], k2)
                    queries = jnp.concatenate([bias[...], qt], 0)
                scores = dot_nn(keys, queries)
                top = jnp.max(scores, 0, keepdims=True)
                weights = jnp.exp(scores - top).astype(BF16)
                exp_s[col, 2 * pair + n] = weights
                sums = dot_nn(jnp.concatenate([vt_s[feats], ones], 0), weights)
                inv = 1.0 / sums[64:65]
                inv_s[col, 2 * pair + n] = jnp.broadcast_to(inv, (8, LEN))
                at_s[col, feats] = (sums[:64] * inv).astype(BF16)
            return carry

        for pair in range(4):
            heads(pair, 0)
        send_a[col] = dot_nt(eye[...], at_s[col]).astype(BF16)

    def attend_back(col):
        x = col_n[col]
        v_s[...] = dot_nn(x, wv[...]).astype(BF16)
        kt_s[...] = dot_nt(wkt[...], x).astype(BF16)
        arrived(0, col, col_g)
        gt_s[...] = dot_nt(wo[...], col_g[col]).astype(BF16)

        def heads(pair, carry):
            for n in range(2):
                lanes, feats = pair_of(pair, n)
                v2, gt = v_s[:, lanes], gt_s[feats]
                grads = jnp.concatenate([none, gt] if n else [gt, none], 0)
                grad_p = dot_nn(v2, grads)
                gtf = gt.astype(F32)
                centre = jnp.sum(at_s[col, feats].astype(F32) * gtf, 0, keepdims=True)
                weights = exp_s[col, 2 * pair + n]
                inv = inv_s[col, 2 * pair + n][0:1]
                grad_s = (weights.astype(F32) * (grad_p - centre)).astype(BF16)
                gq_s[feats] = (dot_nn(kt_s[feats], grad_s) * (inv * 0.125)).astype(BF16)
                gv_s[feats] = dot_nt((gtf * inv).astype(BF16), weights).astype(BF16)
                query = (qt_s[col, feats].astype(F32) * inv).astype(BF16)
                gk_s[feats] = dot_nt(query, grad_s).astype(BF16)
            return carry

        for pair in range(4):
            heads(pair, 0)
        grads_t = dot_nn(wq[...], gq_s[...]) + dot_nn(wk[...], gk_s[...])
        grads_t = (grads_t + dot_nn(wv[...], gv_s[...])).astype(BF16)
        send_b[col] = dot_nt(eye[...], grads_t).astype(BF16)

    def project(k):
        arrived(3, k, ret_a)
        att = dot_nn(swap[...], ret_a[k]).astype(BF16)
        whole = filt[k].astype(F32) + dot_nn(att, wo[...])
        out[:, k] = whole.astype(BF16).reshape(DEP, 16, WID)
        cp = pltpu.make_async_copy(out.at[:, k], out_h.at[:, k], store_sem.at[0, k])
        cp.start()
        return cp

    attend(0)
    exchange(3, 0, send_a, ret_a)
    attend(1)
    attend_back(0)
    exchange(2, 0, send_b, ret_b)
    attend_back(1)
    exchange(2, 1, send_b, ret_b)
    exchange(3, 1, send_a, ret_a)
    stores = [project(0)]

    depth = []
    sides = []
    for k in range(2):
        arrived(2, k, ret_b)
        unit_grad = dot_nn(swap[...], ret_b[k]) * gain_row
        xhat = unit[k]
        mean = jnp.sum(unit_grad, -1, keepdims=True) * (1.0 / WID)
        along = jnp.sum(unit_grad * xhat, -1, keepdims=True) * (1.0 / WID)
        inv = scale[k][:, 0:1]
        rest = go[:, k].reshape(LEN, WID).astype(F32)
        rounded = (rest + inv * (unit_grad - mean - xhat * along)).astype(BF16)
        grad_f[:, k] = rounded.reshape(DEP, 16, WID)
        values = rounded.astype(F32).reshape(DEP, 2, WIN, WID)
        pad[1 : 1 + DEP, 1 + 2 * k : 3 + 2 * k] = values
        edge[1, k] = values[:, k].reshape(DEP * WIN, WID).astype(BF16)
        new = halo_side(1, k), halo_depth(1, grad_f, k)
        start(new[1] + new[0])
        sides.append(new[0])
        depth.append(new[1])

    stores.append(project(1))

    def adjoint(k, first, count):
        def one(d, carry):
            conv = [
                conv_row(pad, taps, d, h, True) + pad[d + 1, h + 1]
                for h in (2 * k, 2 * k + 1)
            ]
            gt[d, k] = jnp.concatenate(conv, 0).astype(BF16)
            return carry

        lax.fori_loop(first, first + count, one, 0)

    finish(sides[0])
    rim_side(1, 1)
    adjoint(1, 1, DEP - 2)
    for k in range(2):
        finish(depth[k])
        rim_depth(1, k)
    adjoint(1, 0, 1)
    adjoint(1, DEP - 1, 1)
    cp = pltpu.make_async_copy(gt.at[:, 1], grad_h.at[:, 1], store_sem.at[1, 1])
    cp.start()
    stores.append(cp)
    finish(sides[1])
    rim_side(1, 0)
    adjoint(0, 0, DEP)
    cp = pltpu.make_async_copy(gt.at[:, 0], grad_h.at[:, 0], store_sem.at[1, 0])
    cp.start()
    stores.append(cp)
    for kind, src in enumerate((send_g, send_n, send_b, send_a)):
        for col in range(PER):
            sent(kind, col, src)
    finish(stores)


def body(tokens, conv_weight, gain, bands, w_query, w_key, w_value, w_out, grad_out):
    whole = (DEP, 2, 16, WID)
    pair = (PER, LEN, WID)
    hbm = pl.BlockSpec(memory_space=pltpu.HBM)
    scratch = [
        pltpu.SMEM((2, 4), jnp.int32),
        pltpu.VMEM((27, WID), BF16),
        pltpu.VMEM((1, WID), F32),
        pltpu.VMEM(whole, BF16), pltpu.VMEM(whole, BF16),
        *[pltpu.VMEM((WID, WID), BF16) for _ in range(7)],
        pltpu.VMEM((27, WIN, WID), F32),
        pltpu.VMEM((DEP + 2, HGT + 2, WIN, WID), F32),
        pltpu.VMEM((2, 2, DEP * WIN, WID), BF16),
        pltpu.VMEM((2, 2, 2, 16, WID), BF16),
        pltpu.VMEM((2, 2, DEP * WIN, WID), BF16),
        pltpu.VMEM((2, 2, 2, 16, WID), BF16),
        *[pltpu.VMEM(pair, BF16) for _ in range(8)],
        pltpu.VMEM((LEN, LEN), BF16), pltpu.VMEM((LEN, LEN), BF16),
        pltpu.VMEM((64, LEN), BF16), pltpu.VMEM((LEN, 128), BF16),
        pltpu.VMEM(pair, BF16), pltpu.VMEM(pair, BF16),
        pltpu.VMEM(pair, F32),
        pltpu.VMEM((PER, LEN, 128), F32),
        *[pltpu.VMEM(whole, BF16) for _ in range(3)],
        *[pltpu.VMEM((LEN, WID), BF16) for _ in range(2)],
        pltpu.VMEM((PER, WID, LEN), BF16),
        *[pltpu.VMEM((WID, LEN), BF16) for _ in range(3)],
        pltpu.VMEM((PER, WID, LEN), BF16),
        *[pltpu.VMEM((WID, LEN), BF16) for _ in range(3)],
        pltpu.VMEM((PER, 8, LEN, LEN), BF16),
        pltpu.VMEM((PER, 8, 8, LEN), F32),
        pltpu.SemaphoreType.DMA((9,)),
        pltpu.SemaphoreType.DMA((2, 2, 5)), pltpu.SemaphoreType.DMA((2, 2, 5)),
        pltpu.SemaphoreType.DMA((4, PER)), pltpu.SemaphoreType.DMA((4, PER)),
        pltpu.SemaphoreType.DMA((2, 2)),
    ]
    out, grad = pl.pallas_call(
        kernel,
        out_shape=(jax.ShapeDtypeStruct(whole, BF16), jax.ShapeDtypeStruct(whole, BF16)),
        in_specs=[hbm] * 9,
        out_specs=(hbm, hbm),
        scratch_shapes=scratch,
        compiler_params=pltpu.CompilerParams(
            collective_id=0, has_side_effects=True, vmem_limit_bytes=60 * 2**20
        ),
        name="sublayer",
    )(
        bands.T, conv_weight, gain.reshape(1, WID), tokens.reshape(whole),
        grad_out.reshape(whole), w_query, w_key, w_value, w_out,
    )
    return out.reshape(tokens.shape), grad.reshape(tokens.shape)


def solution(mesh):
    slab = P("grp", "inner", None, None)
    in_specs = (slab, P(), P(), P(), P(), P(), P(), P(), slab)
    return jax.shard_map(
        body, mesh=mesh, in_specs=in_specs, out_specs=(slab, slab), check_vma=False
    )
```

time: 83.6 us -> 66.1 us (0.79)
  Pallas kernels: 72.6 us -> 62.5 us
  local copies, waits for them, and re-layouts: 9.35 us -> 2.74 us
    pallas_call x1, Pallas kernels: 72.6 us -> 62.5 us  [body(): pl.pallas_call(kernel, out_shape=(jax.ShapeDtypeStruct(whole, BF16), jax....]
    unnamed x21 -> x4, local copies, waits for them, and re-layouts: 9.35 us -> 2.74 us
where the time goes in v2:
time: 66.1 us; the launch traced here: 65.9 us
  Pallas kernels  62.5 us (95%)
  local copies, waits for them, and re-layouts  2.74 us (4%)
    pallas_call x1, Pallas kernels, body(): pl.pallas_call(kernel, out_shape=(jax.ShapeDtypeStruct(whole, BF16), jax....  62.5 us
    unnamed x4, local copies, waits for them, and re-layouts  2.74 us

profile of v2, /device:TPU:1, one launch (start us, length us, event | category | flops | bytes accessed | tf_op | source)
XLA Modules:
  0.0 65.9 jit_solution(15053909257431488887)
XLA Ops:
  0.6 62.5 %sublayer.1 = (bf16[16,2,16,512]{3,2,1,0:T(8,128)(2,1)}, bf16[16,2,16,512]{3,2,1,0:T(8,128)(2,1)}) custom-call(s32[2,4]{1,0:T(2,128)} %bitcast.11, bf16[27,512]{1,0:T(8,128)(2,1)} %conv_h.1, f32[1,512]{1,0:T(1,128)} %bitcast.10, bf16[16,2,16,512]{3,2,1,0:T(8,128)(2,1)} %bitcast.6, bf16[16,2,16,512]{3,2,1,0:T(8,128)(2,1)} %bitcast.7, bf16[512,512]{1,0:T(8,128)(2,1)} %wq_h.1, ...), custom_call_target="tpu_custom_call" | custom-call | tf_op jit(solution)/shard_map/sublayer/pallas_call | solution.py:441
  63.2 0.0 copy-start
  63.2 1.9 %copy.13 = bf16[16,4,8,512]{3,2,1,0:T(8,128)(2,1)} copy(bf16[16,4,8,512]{3,2,1,0:T(8,128)(2,1)} %bitcast.9) | data formatting | bytes 1048576
  65.1 0.0 copy-done
  65.1 0.8 %copy.14 = bf16[16,4,8,512]{3,2,1,0:T(8,128)(2,1)} copy(bf16[16,4,8,512]{3,2,1,0:T(8,128)(2,1)S(1)} %bitcast.8) | data formatting | bytes 1048576
Async XLA Ops:
  63.2 2.0 %copy-start = (bf16[16,2,16,512]{3,2,1,0:T(8,128)(2,1)S(1)}, bf16[16,2,16,512]{3,2,1,0:T(8,128)(2,1)}, u32[]{:S(2)}) copy-start(bf16[16,2,16,512]{3,2,1,0:T(8,128)(2,1)} %get-tuple-element.5) | copy-start | bytes 1572868

commit v3 on v2

--- a/solution.py
+++ b/solution.py
@@ -24,6 +24,10 @@
 
 def dot_nt(a, b):
     return lax.dot_general(a, b, (((1,), (1,)), ((), ())), preferred_element_type=F32)
+
+
+def dot_tn(a, b):
+    return lax.dot_general(a, b, (((0,), (0,)), ((), ())), preferred_element_type=F32)
 
 
 def iota(shape, dim):
@@ -50,7 +54,7 @@
     bands, conv_w, gain, tok, go, wq, wk, wv, wo, wqt, wkt, wvt, taps, pad, edge,
     rim_d, rim_h, rim_c, send_n, send_g, col_n, col_g, send_a, send_b, ret_a, ret_b,
     swap, eye, bias, hot, filt, normed, unit, scale, grad_f, out, gt,
-    k_s, v_s, qt_s, kt_s, vt_s, gt_s, at_s, gq_s, gk_s, gv_s, exp_s, inv_s,
+    k_s, v_s, qt_s, kt_s, vt_s, gt_s, at_s, gq_s, gk_s, gv_s, exp_s, inv_s, grad_s, mid,
     load_sem, halo_ss, halo_rs, a2a_ss, a2a_rs, store_sem,
 ):
     g = lax.axis_index("grp")
@@ -172,6 +176,22 @@
             src.at[col, rows], src.at[col, rows], a2a_ss.at[kind, col]
         ).wait()
 
+    def filtered(d, h, flip):
+        return conv_row(pad, taps, d, h, flip) + pad[d + 1, h + 1]
+
+    def middle(flip, first, count):
+        def one(d, carry):
+            for k in range(2):
+                mid[k, d] = filtered(d, 1 + k, flip)
+            return carry
+
+        lax.fori_loop(first, first + count, one, 0, unroll=2 if count > 1 else 1)
+
+    def both_rows(d, k, flip):
+        outer = filtered(d, 3 * k, flip)
+        rows = [mid[k, d], outer] if k else [outer, mid[k, d]]
+        return jnp.concatenate(rows, 0).astype(BF16)
+
     loads[0].wait()
 
     def fill(d, carry):
@@ -194,7 +214,6 @@
     loads[2].wait()
     for k in range(2):
         send_g[k] = dot_nn(swap[...], go[:, k].reshape(LEN, WID)).astype(BF16)
-    exchange(0, 0, send_g, col_g)
 
     loads[1].wait()
     conv_f = conv_w[...].astype(F32)
@@ -219,9 +238,12 @@
         cp.wait()
     gain_row = gain[...]
 
+    middle(False, 1, DEP - 2)
     finish(depth)
     for k in range(2):
         rim_depth(0, k)
+    middle(False, 0, 1)
+    middle(False, DEP - 1, 1)
 
     for k in range(2):
         finish(top if k else low)
@@ -229,14 +251,10 @@
 
         def forward(d, carry, k=k):
             rows = pl.ds(pl.multiple_of(d * 16, 16), 16)
-            conv = [
-                conv_row(pad, taps, d, h, False) + pad[d + 1, h + 1]
-                for h in (2 * k, 2 * k + 1)
-            ]
-            filt[k, rows] = jnp.concatenate(conv, 0).astype(BF16)
+            filt[k, rows] = both_rows(d, k, False)
             return carry
 
-        lax.fori_loop(0, DEP, forward, 0)
+        lax.fori_loop(0, DEP, forward, 0, unroll=2)
         for n in range(LEN // 64):
             rows = slice(n * 64, (n + 1) * 64)
             vals = filt[k, rows].astype(F32)
@@ -250,6 +268,7 @@
         send_n[k] = dot_nn(swap[...], normed[k]).astype(BF16)
         exchange(1, k, send_n, col_n)
 
+    exchange(0, 0, send_g, col_g)
     exchange(0, 1, send_g, col_g)
 
     for src, dst in ((wq, wqt), (wk, wkt), (wv, wvt)):
@@ -261,10 +280,9 @@
     none = jnp.zeros(slim, BF16)
     ones = jnp.ones((16, LEN), BF16)
 
-    def pair_of(pair, n):
-        lanes = pl.ds(pair * 128, 128)
-        feats = pl.ds(pair * 128 + n * 64, 64)
-        return lanes, feats
+    def part_of(head):
+        first = head // 2 * 128
+        return slice(first, first + 128), slice(head * 64, head * 64 + 64)
 
     def attend(col):
         arrived(1, col, col_n)
@@ -274,29 +292,25 @@
         qt_s[col] = query.astype(BF16)
         vt_s[...] = dot_nt(wvt[...], x).astype(BF16)
 
-        def heads(pair, carry):
-            for n in range(2):
-                lanes, feats = pair_of(pair, n)
-                k2, qt = k_s[:, lanes], qt_s[col, feats]
-                if n == 0:
-                    keys = jnp.where(low_half, k2, hot[...])
-                    queries = jnp.concatenate([qt, bias[...]], 0)
-                else:
-                    keys = jnp.where(low_half, hot[...], k2)
-                    queries = jnp.concatenate([bias[...], qt], 0)
-                scores = dot_nn(keys, queries)
-                top = jnp.max(scores, 0, keepdims=True)
-                weights = jnp.exp(scores - top).astype(BF16)
-                exp_s[col, 2 * pair + n] = weights
-                sums = dot_nn(jnp.concatenate([vt_s[feats], ones], 0), weights)
-                inv = 1.0 / sums[64:65]
-                inv_s[col, 2 * pair + n] = jnp.broadcast_to(inv, (8, LEN))
-                at_s[col, feats] = (sums[:64] * inv).astype(BF16)
-            return carry
-
-        for pair in range(4):
-            heads(pair, 0)
-        send_a[col] = dot_nt(eye[...], at_s[col]).astype(BF16)
+        for head in range(8):
+            lanes, feats = part_of(head)
+            k2, qt = k_s[:, lanes], qt_s[col, feats]
+            if head % 2 == 0:
+                keys = jnp.where(low_half, k2, hot[...])
+                queries = jnp.concatenate([qt, bias[...]], 0)
+            else:
+                keys = jnp.where(low_half, hot[...], k2)
+                queries = jnp.concatenate([bias[...], qt], 0)
+            scores = dot_nn(keys, queries)
+            peak = jnp.max(scores, 0, keepdims=True)
+            exp_s[col, head] = jnp.exp(scores - peak).astype(BF16)
+        for head in range(8):
+            lanes, feats = part_of(head)
+            sums = dot_nn(jnp.concatenate([vt_s[feats], ones], 0), exp_s[col, head])
+            inv = 1.0 / sums[64:65]
+            inv_s[col, head] = jnp.broadcast_to(inv, (8, LEN))
+            at_s[col, feats] = (sums[:64] * inv).astype(BF16)
+        send_a[col] = at_s[col].T
 
     def attend_back(col):
         x = col_n[col]
@@ -305,28 +319,27 @@
         arrived(0, col, col_g)
         gt_s[...] = dot_nt(wo[...], col_g[col]).astype(BF16)
 
-        def heads(pair, carry):
-            for n in range(2):
-                lanes, feats = pair_of(pair, n)
-                v2, gt = v_s[:, lanes], gt_s[feats]
-                grads = jnp.concatenate([none, gt] if n else [gt, none], 0)
-                grad_p = dot_nn(v2, grads)
-                gtf = gt.astype(F32)
-                centre = jnp.sum(at_s[col, feats].astype(F32) * gtf, 0, keepdims=True)
-                weights = exp_s[col, 2 * pair + n]
-                inv = inv_s[col, 2 * pair + n][0:1]
-                grad_s = (weights.astype(F32) * (grad_p - centre)).astype(BF16)
-                gq_s[feats] = (dot_nn(kt_s[feats], grad_s) * (inv * 0.125)).astype(BF16)
-                gv_s[feats] = dot_nt((gtf * inv).astype(BF16), weights).astype(BF16)
-                query = (qt_s[col, feats].astype(F32) * inv).astype(BF16)
-                gk_s[feats] = dot_nt(query, grad_s).astype(BF16)
-            return carry
-
-        for pair in range(4):
-            heads(pair, 0)
-        grads_t = dot_nn(wq[...], gq_s[...]) + dot_nn(wk[...], gk_s[...])
-        grads_t = (grads_t + dot_nn(wv[...], gv_s[...])).astype(BF16)
-        send_b[col] = dot_nt(eye[...], grads_t).astype(BF16)
+        for head in range(8):
+            lanes, feats = part_of(head)
+            v2, gt_h = v_s[:, lanes], gt_s[feats]
+            grads = jnp.concatenate([none, gt_h] if head % 2 else [gt_h, none], 0)
+            grad_p = dot_nn(v2, grads)
+            dots = at_s[col, feats].astype(F32) * gt_h.astype(F32)
+            centre = jnp.sum(dots, 0, keepdims=True)
+            weights = exp_s[col, head].astype(F32)
+            grad_s[head] = (weights * (grad_p - centre)).astype(BF16)
+        for head in range(8):
+            lanes, feats = part_of(head)
+            inv = inv_s[col, head][0:1]
+            gt_h = (gt_s[feats].astype(F32) * inv).astype(BF16)
+            gv_s[feats] = dot_nt(gt_h, exp_s[col, head]).astype(BF16)
+            query = (qt_s[col, feats].astype(F32) * inv).astype(BF16)
+            gk_s[feats] = dot_nt(query, grad_s[head]).astype(BF16)
+            key = dot_nn(kt_s[feats], grad_s[head])
+            gq_s[feats] = (key * (inv * 0.125)).astype(BF16)
+        send_b[col] = (
+            dot_tn(gq_s[...], wqt[...]) + dot_tn(gk_s[...], wkt[...]) + dot_tn(gv_s[...], wvt[...])
+        ).astype(BF16)
 
     def project(k):
         arrived(3, k, ret_a)
@@ -340,11 +353,11 @@
     attend(0)
     exchange(3, 0, send_a, ret_a)
     attend(1)
+    exchange(3, 1, send_a, ret_a)
     attend_back(0)
     exchange(2, 0, send_b, ret_b)
     attend_back(1)
     exchange(2, 1, send_b, ret_b)
-    exchange(3, 1, send_a, ret_a)
     stores = [project(0)]
 
     depth = []
@@ -371,23 +384,21 @@
 
     def adjoint(k, first, count):
         def one(d, carry):
-            conv = [
-                conv_row(pad, taps, d, h, True) + pad[d + 1, h + 1]
-                for h in (2 * k, 2 * k + 1)
-            ]
-            gt[d, k] = jnp.concatenate(conv, 0).astype(BF16)
+            gt[d, k] = both_rows(d, k, True)
             return carry
 
-        lax.fori_loop(first, first + count, one, 0)
-
+        lax.fori_loop(first, first + count, one, 0, unroll=2 if count > 1 else 1)
+
+    middle(True, 1, DEP - 2)
     finish(sides[0])
     rim_side(1, 1)
     adjoint(1, 1, DEP - 2)
     for k in range(2):
         finish(depth[k])
         rim_depth(1, k)
-    adjoint(1, 0, 1)
-    adjoint(1, DEP - 1, 1)
+    for d in (0, DEP - 1):
+        middle(True, d, 1)
+        adjoint(1, d, 1)
     cp = pltpu.make_async_copy(gt.at[:, 1], grad_h.at[:, 1], store_sem.at[1, 1])
     cp.start()
     stores.append(cp)
@@ -401,6 +412,24 @@
         for col in range(PER):
             sent(kind, col, src)
     finish(stores)
+
+
+def hand_over(out_in, grad_in, out_ref, grad_ref, held, in_sem, out_sem):
+    moves = []
+    for n, (src, dst) in enumerate(((out_in, out_ref), (grad_in, grad_ref))):
+        for half in range(2):
+            rows = pl.ds(half * DEP // 2, DEP // 2)
+            moves.append((
+                pltpu.make_async_copy(src.at[rows], held.at[n, rows], in_sem.at[n, half]),
+                pltpu.make_async_copy(held.at[n, rows], dst.at[rows], out_sem.at[n, half]),
+            ))
+    for load, _ in moves:
+        load.start()
+    for load, store in moves:
+        load.wait()
+        store.start()
+    for _, store in moves:
+        store.wait()
 
 
 def body(tokens, conv_weight, gain, bands, w_query, w_key, w_value, w_out, grad_out):
@@ -433,12 +462,14 @@
         *[pltpu.VMEM((WID, LEN), BF16) for _ in range(3)],
         pltpu.VMEM((PER, 8, LEN, LEN), BF16),
         pltpu.VMEM((PER, 8, 8, LEN), F32),
+        pltpu.VMEM((8, LEN, LEN), BF16),
+        pltpu.VMEM((2, DEP, WIN, WID), F32),
         pltpu.SemaphoreType.DMA((9,)),
         pltpu.SemaphoreType.DMA((2, 2, 5)), pltpu.SemaphoreType.DMA((2, 2, 5)),
         pltpu.SemaphoreType.DMA((4, PER)), pltpu.SemaphoreType.DMA((4, PER)),
         pltpu.SemaphoreType.DMA((2, 2)),
     ]
-    out, grad = pl.pallas_call(
+    made = pl.pallas_call(
         kernel,
         out_shape=(jax.ShapeDtypeStruct(whole, BF16), jax.ShapeDtypeStruct(whole, BF16)),
         in_specs=[hbm] * 9,
@@ -452,6 +483,18 @@
         bands.T, conv_weight, gain.reshape(1, WID), tokens.reshape(whole),
         grad_out.reshape(whole), w_query, w_key, w_value, w_out,
     )
+    out, grad = pl.pallas_call(
+        hand_over,
+        out_shape=(jax.ShapeDtypeStruct(whole, BF16), jax.ShapeDtypeStruct(whole, BF16)),
+        in_specs=[hbm] * 2,
+        out_specs=(hbm, hbm),
+        scratch_shapes=[
+            pltpu.VMEM((2, *whole), BF16),
+            pltpu.SemaphoreType.DMA((2, 2)), pltpu.SemaphoreType.DMA((2, 2)),
+        ],
+        compiler_params=pltpu.CompilerParams(vmem_limit_bytes=60 * 2**20),
+        name="hand_over",
+    )(*made)
     return out.reshape(tokens.shape), grad.reshape(tokens.shape)
 
 

time: 66.1 us -> 61.3 us (0.927)
  local copies, waits for them, and re-layouts: 2.74 us -> 0 us
  Pallas kernels: 62.5 us -> 60.5 us
    pallas_call x1, Pallas kernels: 62.5 us -> 58.6 us  [body(): pl.pallas_call(kernel, out_shape=(jax.ShapeDtypeStruct(whole, BF16), jax....]
    unnamed x4 -> x0, local copies, waits for them, and re-layouts: 2.74 us -> none
    pallas_call x0 -> x1, Pallas kernels: none -> 1.98 us  [body(): pl.pallas_call(hand_over, out_shape=(jax.ShapeDtypeStruct(whole, BF16), j...]
where the time goes in v3:
time: 61.3 us; the launch traced here: 61.2 us
  Pallas kernels  60.5 us (99%)
  between operations  0.64 us (1%)
    pallas_call x1, Pallas kernels, body(): pl.pallas_call(kernel, out_shape=(jax.ShapeDtypeStruct(whole, BF16), jax....  58.6 us
    pallas_call x1, Pallas kernels, body(): pl.pallas_call(hand_over, out_shape=(jax.ShapeDtypeStruct(whole, BF16), j...  1.98 us

profile of v3, /device:TPU:1, one launch (start us, length us, event | category | flops | bytes accessed | tf_op | source)
XLA Modules:
  0.0 61.2 jit_solution(1053832147831388205)
XLA Ops:
  0.6 58.6 %sublayer.1 = (bf16[16,2,16,512]{3,2,1,0:T(8,128)(2,1)}, bf16[16,2,16,512]{3,2,1,0:T(8,128)(2,1)}) custom-call(s32[2,4]{1,0:T(2,128)} %bitcast.9, bf16[27,512]{1,0:T(8,128)(2,1)} %conv_h.1, f32[1,512]{1,0:T(1,128)} %bitcast.8, bf16[16,2,16,512]{3,2,1,0:T(8,128)(2,1)} %bitcast.6, bf16[16,2,16,512]{3,2,1,0:T(8,128)(2,1)} %bitcast.7, bf16[512,512]{1,0:T(8,128)(2,1)} %wq_h.1, ...), custom_call_target="tpu_custom_call" | custom-call | tf_op jit(solution)/shard_map/sublayer/pallas_call | solution.py:472
  59.2 2.0 %hand_over.1 = (bf16[16,2,16,512]{3,2,1,0:T(8,128)(2,1)}, bf16[16,2,16,512]{3,2,1,0:T(8,128)(2,1)}) custom-call(bf16[16,2,16,512]{3,2,1,0:T(8,128)(2,1)} %get-tuple-element.6.out_in, bf16[16,2,16,512]{3,2,1,0:T(8,128)(2,1)} %get-tuple-element.7.grad_in), custom_call_target="tpu_custom_call" | custom-call | tf_op jit(solution)/shard_map/hand_over/pallas_call | solution.py:486

commit v4 on v3

--- a/solution.py
+++ b/solution.py
@@ -65,7 +65,8 @@
     up_i, dn_i = lax.rem(i + 1, ni), lax.rem(i + ni - 1, ni)
 
     pairs = (
-        (tok_h, tok), (conv_h, conv_w), (go_h, go), (bands_h, bands), (gain_h, gain),
+        (tok_h.at[:, 1], tok.at[:, 1]), (tok_h.at[:, 0], tok.at[:, 0]),
+        (conv_h, conv_w), (go_h, go), (bands_h, bands), (gain_h, gain),
         (wq_h, wq), (wk_h, wk), (wv_h, wv), (wo_h, wo),
     )
     loads = [
@@ -192,35 +193,39 @@
         rows = [mid[k, d], outer] if k else [outer, mid[k, d]]
         return jnp.concatenate(rows, 0).astype(BF16)
 
-    loads[0].wait()
-
     def fill(d, carry):
         pad[1 + d, 1 : 1 + HGT] = tok[d].reshape(COLS, WID).astype(F32).reshape(HGT, WIN, WID)
         return carry
 
-    lax.fori_loop(0, DEP, fill, 0)
-    for k in range(2):
-        edge[0, k] = pad[1 : 1 + DEP, 1 + 3 * k].reshape(DEP * WIN, WID).astype(BF16)
+    def stage(k):
+        rows = tok[:, k].astype(F32).reshape(DEP, 2, WIN, WID)
+        edge[0, k] = rows[:, k].reshape(DEP * WIN, WID).astype(BF16)
+
+    loads[0].wait()
+    stage(1)
+    loads[1].wait()
+    stage(0)
     pl.semaphore_wait(barrier, ng - 1 + len(sides))
     depth = halo_depth(0, tok, 0) + halo_depth(0, tok, 1)
     low, top = halo_side(0, 1), halo_side(0, 0)
     start(depth + low + top)
+    lax.fori_loop(0, DEP, fill, 0)
 
     square = (LEN, LEN)
     row, lane = iota(square, 0), iota(square, 1)
     swap[...] = jnp.where(lane == (row & 15) * 16 + (row >> 4), 1.0, 0.0).astype(BF16)
     eye[...] = jnp.where(row == lane, 1.0, 0.0).astype(BF16)
 
-    loads[2].wait()
+    loads[3].wait()
     for k in range(2):
         send_g[k] = dot_nn(swap[...], go[:, k].reshape(LEN, WID)).astype(BF16)
 
-    loads[1].wait()
+    loads[2].wait()
     conv_f = conv_w[...].astype(F32)
     for n in range(27):
         taps[n] = jnp.broadcast_to(conv_f[n : n + 1], (WIN, WID))
 
-    loads[3].wait()
+    loads[4].wait()
     slim = (64, LEN)
     key_block = iota(slim, 0)
     query_block = iota(slim, 1) >> 6
@@ -234,7 +239,7 @@
     wide = (LEN, 128)
     hot[...] = jnp.where((iota(wide, 1) & 63) == (iota(wide, 0) >> 6), 1.0, 0.0).astype(BF16)
 
-    for cp in loads[4:]:
+    for cp in loads[5:]:
         cp.wait()
     gain_row = gain[...]
 
@@ -247,6 +252,8 @@
 
     for k in range(2):
         finish(top if k else low)
+        if k == 0:
+            exchange(0, 0, send_g, col_g)
         rim_side(0, k)
 
         def forward(d, carry, k=k):
@@ -268,7 +275,6 @@
         send_n[k] = dot_nn(swap[...], normed[k]).astype(BF16)
         exchange(1, k, send_n, col_n)
 
-    exchange(0, 0, send_g, col_g)
     exchange(0, 1, send_g, col_g)
 
     for src, dst in ((wq, wqt), (wk, wkt), (wv, wvt)):
@@ -464,7 +470,7 @@
         pltpu.VMEM((PER, 8, 8, LEN), F32),
         pltpu.VMEM((8, LEN, LEN), BF16),
         pltpu.VMEM((2, DEP, WIN, WID), F32),
-        pltpu.SemaphoreType.DMA((9,)),
+        pltpu.SemaphoreType.DMA((10,)),
         pltpu.SemaphoreType.DMA((2, 2, 5)), pltpu.SemaphoreType.DMA((2, 2, 5)),
         pltpu.SemaphoreType.DMA((4, PER)), pltpu.SemaphoreType.DMA((4, PER)),
         pltpu.SemaphoreType.DMA((2, 2)),

time: 61.3 us -> 60.9 us (level)
  no operation moved by 1% of the time
where the time goes in v4:
time: 60.9 us; the launch traced here: 60.7 us
  Pallas kernels  60.1 us (99%)
  between operations  0.64 us (1%)
    pallas_call x1, Pallas kernels, body(): pl.pallas_call(kernel, out_shape=(jax.ShapeDtypeStruct(whole, BF16), jax....  58.1 us
    pallas_call x1, Pallas kernels, body(): pl.pallas_call(hand_over, out_shape=(jax.ShapeDtypeStruct(whole, BF16), j...  1.98 us

profile of v4, /device:TPU:1, one launch (start us, length us, event | category | flops | bytes accessed | tf_op | source)
XLA Modules:
  0.0 60.7 jit_solution(9868779911293786358)
XLA Ops:
  0.6 58.1 %sublayer.1 = (bf16[16,2,16,512]{3,2,1,0:T(8,128)(2,1)}, bf16[16,2,16,512]{3,2,1,0:T(8,128)(2,1)}) custom-call(s32[2,4]{1,0:T(2,128)} %bitcast.9, bf16[27,512]{1,0:T(8,128)(2,1)} %conv_h.1, f32[1,512]{1,0:T(1,128)} %bitcast.8, bf16[16,2,16,512]{3,2,1,0:T(8,128)(2,1)} %bitcast.6, bf16[16,2,16,512]{3,2,1,0:T(8,128)(2,1)} %bitcast.7, bf16[512,512]{1,0:T(8,128)(2,1)} %wq_h.1, ...), custom_call_target="tpu_custom_call" | custom-call | tf_op jit(solution)/shard_map/sublayer/pallas_call | solution.py:478
  58.8 2.0 %hand_over.1 = (bf16[16,2,16,512]{3,2,1,0:T(8,128)(2,1)}, bf16[16,2,16,512]{3,2,1,0:T(8,128)(2,1)}) custom-call(bf16[16,2,16,512]{3,2,1,0:T(8,128)(2,1)} %get-tuple-element.6.out_in, bf16[16,2,16,512]{3,2,1,0:T(8,128)(2,1)} %get-tuple-element.7.grad_in), custom_call_target="tpu_custom_call" | custom-call | tf_op jit(solution)/shard_map/hand_over/pallas_call | solution.py:492

commit v5 on v4

--- a/solution.py
+++ b/solution.py
@@ -410,10 +410,12 @@
     stores.append(cp)
     finish(sides[1])
     rim_side(1, 0)
-    adjoint(0, 0, DEP)
-    cp = pltpu.make_async_copy(gt.at[:, 0], grad_h.at[:, 0], store_sem.at[1, 0])
-    cp.start()
-    stores.append(cp)
+    for n in range(2):
+        adjoint(0, n * DEP // 2, DEP // 2)
+        rows = pl.ds(n * DEP // 2, DEP // 2)
+        cp = pltpu.make_async_copy(gt.at[rows, 0], grad_h.at[rows, 0], store_sem.at[2, n])
+        cp.start()
+        stores.append(cp)
     for kind, src in enumerate((send_g, send_n, send_b, send_a)):
         for col in range(PER):
             sent(kind, col, src)
@@ -423,11 +425,11 @@
 def hand_over(out_in, grad_in, out_ref, grad_ref, held, in_sem, out_sem):
     moves = []
     for n, (src, dst) in enumerate(((out_in, out_ref), (grad_in, grad_ref))):
-        for half in range(2):
-            rows = pl.ds(half * DEP // 2, DEP // 2)
+        for part in range(4):
+            rows = pl.ds(part * DEP // 4, DEP // 4)
             moves.append((
-                pltpu.make_async_copy(src.at[rows], held.at[n, rows], in_sem.at[n, half]),
-                pltpu.make_async_copy(held.at[n, rows], dst.at[rows], out_sem.at[n, half]),
+                pltpu.make_async_copy(src.at[rows], held.at[n, rows], in_sem.at[n, part]),
+                pltpu.make_async_copy(held.at[n, rows], dst.at[rows], out_sem.at[n, part]),
             ))
     for load, _ in moves:
         load.start()
@@ -473,7 +475,7 @@
         pltpu.SemaphoreType.DMA((10,)),
         pltpu.SemaphoreType.DMA((2, 2, 5)), pltpu.SemaphoreType.DMA((2, 2, 5)),
         pltpu.SemaphoreType.DMA((4, PER)), pltpu.SemaphoreType.DMA((4, PER)),
-        pltpu.SemaphoreType.DMA((2, 2)),
+        pltpu.SemaphoreType.DMA((3, 2)),
     ]
     made = pl.pallas_call(
         kernel,
@@ -496,7 +498,7 @@
         out_specs=(hbm, hbm),
         scratch_shapes=[
             pltpu.VMEM((2, *whole), BF16),
-            pltpu.SemaphoreType.DMA((2, 2)), pltpu.SemaphoreType.DMA((2, 2)),
+            pltpu.SemaphoreType.DMA((2, 4)), pltpu.SemaphoreType.DMA((2, 4)),
         ],
         compiler_params=pltpu.CompilerParams(vmem_limit_bytes=60 * 2**20),
         name="hand_over",

time: 60.9 us -> 61 us (level)
  no operation moved by 1% of the time
where the time goes in v5:
time: 61 us; the launch traced here: 60.8 us
  Pallas kernels  60.2 us (99%)
  between operations  0.64 us (1%)
    pallas_call x1, Pallas kernels, body(): pl.pallas_call(kernel, out_shape=(jax.ShapeDtypeStruct(whole, BF16), jax....  58.1 us
    pallas_call x1, Pallas kernels, body(): pl.pallas_call(hand_over, out_shape=(jax.ShapeDtypeStruct(whole, BF16), j...  2.09 us

profile of v5, /device:TPU:1, one launch (start us, length us, event | category | flops | bytes accessed | tf_op | source)
XLA Modules:
  0.0 60.8 jit_solution(15869482438152032677)
XLA Ops:
  0.6 58.1 %sublayer.1 = (bf16[16,2,16,512]{3,2,1,0:T(8,128)(2,1)}, bf16[16,2,16,512]{3,2,1,0:T(8,128)(2,1)}) custom-call(s32[2,4]{1,0:T(2,128)} %bitcast.9, bf16[27,512]{1,0:T(8,128)(2,1)} %conv_h.1, f32[1,512]{1,0:T(1,128)} %bitcast.8, bf16[16,2,16,512]{3,2,1,0:T(8,128)(2,1)} %bitcast.6, bf16[16,2,16,512]{3,2,1,0:T(8,128)(2,1)} %bitcast.7, bf16[512,512]{1,0:T(8,128)(2,1)} %wq_h.1, ...), custom_call_target="tpu_custom_call" | custom-call | tf_op jit(solution)/shard_map/sublayer/pallas_call | solution.py:480
  58.7 2.1 %hand_over.1 = (bf16[16,2,16,512]{3,2,1,0:T(8,128)(2,1)}, bf16[16,2,16,512]{3,2,1,0:T(8,128)(2,1)}) custom-call(bf16[16,2,16,512]{3,2,1,0:T(8,128)(2,1)} %get-tuple-element.6.out_in, bf16[16,2,16,512]{3,2,1,0:T(8,128)(2,1)} %get-tuple-element.7.grad_in), custom_call_target="tpu_custom_call" | custom-call | tf_op jit(solution)/shard_map/hand_over/pallas_call | solution.py:494
